TPU v7x, 256 devices: a whole 4x4x8 slice. The times are simulated.
256 devices in a mesh: bead: 16 (over z, core), atom: 16 (over x, y).
Axes of the slice: x: 4, y: 4, z: 8, core: 2. Of those that a mesh axis runs over, the one named last changes fastest.
Arguments:
- positions: float32 [64, 3, 16384], P('bead', None, 'atom'), may hold values from -6 to 6
- momenta: float32 [64, 3, 16384], P('bead', None, 'atom'), may hold values from -6 to 6
- charge: float32 [16384], P('atom'), may hold values from -1 to 1
- masses: float32 [16384], P('atom'), may hold values from 0.5 to 4
- pair_local: int32 [512], P('atom'), may hold values from 0 to 127, as said below
- pair_other: int32 [512], P('atom'), may hold values from 0 to 127, as said below
- pair_count: int32 [16], P('atom'), may hold values from 0 to 32, as said below
Outputs:
- new_positions: float32 [64, 3, 16384], P('bead', None, 'atom')
- new_momenta: float32 [64, 3, 16384], P('bead', None, 'atom')
- spring: float32 [16384], P('atom')
Inputs may be any that keep to these rules, and one draw needn't show every extreme that they name: `pair_local`: the slots of atom block d (slots d * 32 to (d + 1) * 32 - 1) name tiles of that block: d * 8 to (d + 1) * 8 - 1. `pair_other`: each slot's neighbour tile lies within 8 tiles of its tile, counting cyclically over 128 tiles. `pair_count`: the counts of blocks d and d + 8 sum to at most 32.
All inputs are finite; a program needn't handle non-finite values.
Results may differ from a plain program's by a relative error of at most 0.000071.
Values sent between devices are 32-bit elements; how exact they have to be, the bound alone decides.
No kernel may reach another device: no remote copies, remote signals or barrier semaphores. Data moves between devices by JAX's collectives and lax.ppermute only.
A program may use at most 64 MiB of HBM per device.

v0:
```python
import functools
import math

import jax
import jax.numpy as jnp
import numpy as np
from jax import lax
from jax.experimental import pallas as pl
from jax.experimental.pallas import tpu as pltpu
from jax.sharding import PartitionSpec as P

time_step = 1.0
omega_cycle = 1.2
width_sq = 2.0

TILE = 128
BEAD_DEV = 4
TILE_DEV = 8
ATOM_DEV = TILE * TILE_DEV
ROWS = 4 * BEAD_DEV
HALF = TILE // 2
GROUP = 8
SCALE = math.log2(math.e) / (2.0 * width_sq)

VMEM = pl.BlockSpec(memory_space=pltpu.VMEM)
SMEM = pl.BlockSpec(memory_space=pltpu.SMEM)
PARAMS = pltpu.CompilerParams(vmem_limit_bytes=24 * 2**20)


def bead_tables(beads):
    j = np.arange(beads, dtype=np.float64)
    k = np.arange(beads, dtype=np.float64)
    angle = 2.0 * np.pi * j[:, None] * k[None, :] / beads
    middle = beads // 2
    table = np.where(
        k[None, :] == 0,
        np.sqrt(1.0 / beads),
        np.where(
            k[None, :] < middle,
            np.sqrt(2.0 / beads) * np.cos(angle),
            np.where(
                k[None, :] == middle,
                np.sqrt(1.0 / beads) * np.cos(np.pi * j[:, None]),
                np.sqrt(2.0 / beads) * np.sin(angle),
            ),
        ),
    )
    omega = 2.0 * omega_cycle * np.sin(np.pi * k / beads)
    sine = np.sin(omega * time_step)
    reach = np.where(omega > 0, sine / np.where(omega > 0, omega, 1.0), time_step)
    parts = (np.cos(omega * time_step), reach, -omega * sine)
    used = np.diag([1.0, 1.0, 1.0, 0.0])
    return [
        np.kron((table * part[None, :]) @ table.T, used).astype(np.float32)
        for part in parts
    ]


def component(shape):
    return lax.broadcasted_iota(jnp.int32, shape, 0) % 4


def by_bead(out_ref, parts):
    for bead in range(BEAD_DEV):
        for axis in range(4):
            out_ref[4 * bead + axis : 4 * bead + axis + 1, :] = parts[axis][bead : bead + 1]


def split3(x):
    high = x.astype(jnp.bfloat16).astype(jnp.float32)
    rest = x - high
    mid = rest.astype(jnp.bfloat16).astype(jnp.float32)
    return high, mid, rest - mid


def with_norm(block):
    square = block * block
    norm = pltpu.roll(square, 1, 0) + pltpu.roll(square, 2, 0) + pltpu.roll(square, 3, 0)
    return jnp.where(component(block.shape) == 3, -SCALE * norm, block)


def prepare_right(block, first, right_ref, value_ref):
    comp = component(block.shape)
    high, mid, low = split3(with_norm(block))
    ones = jnp.ones((4, ATOM_DEV), jnp.float32)
    charge = block[3:4, :]
    values = split3(charge * jnp.where(comp == 3, 1.0, block))
    for bead in range(BEAD_DEV):
        rows = slice(4 * bead, 4 * bead + 4)
        h, m, l = high[rows], mid[rows], low[rows]
        right = jnp.concatenate([h, m, l, h, m, h, ones, 0.0 * ones], 0).astype(jnp.bfloat16)
        value = jnp.concatenate([v[rows] for v in values] + [0.0 * ones], 0).astype(jnp.bfloat16)
        for tile in range(TILE_DEV):
            lanes = slice(tile * TILE, (tile + 1) * TILE)
            right_ref[first + tile, bead] = right[:, lanes]
            value_ref[first + tile, bead] = value[:, lanes]


def prepare_left(block, left_ref):
    comp = component(block.shape)
    normed = with_norm(block)
    high, mid, low = split3(jnp.where(comp == 3, normed, 2.0 * SCALE * normed))
    for bead in range(BEAD_DEV):
        rows = slice(4 * bead, 4 * bead + 4)
        h, m, l = high[rows], mid[rows], low[rows]
        last = comp[rows] == 3
        h1 = jnp.where(last, 1.0, h)
        m0 = jnp.where(last, 0.0, m)
        l0 = jnp.where(last, 0.0, l)
        norms = jnp.concatenate([h[3:4], m[3:4], l[3:4], jnp.zeros((1, ATOM_DEV), jnp.float32)], 0)
        left = jnp.concatenate([h1, h1, h1, m0, m0, l0, norms, jnp.zeros_like(h)], 0)
        for tile in range(TILE_DEV):
            lanes = slice(tile * TILE, (tile + 1) * TILE)
            left_ref[tile, bead] = left[:, lanes].T.astype(jnp.bfloat16)


def list_slots(near, tiles, local_ref, other_ref, count_ref, list_ref):
    slots = local_ref.shape[0]
    spare = list_ref.shape[0] // 2
    count = count_ref[0]
    swapped = TILE_DEV - (local_ref[0] & TILE_DEV)
    size = jnp.int32(0)
    for slot in range(slots):
        tile = local_ref[slot] & (TILE_DEV - 1)
        place = (other_ref[slot] - local_ref[slot] + tile + TILE_DEV) & (tiles - 1)
        inside = (place >= TILE_DEV) & (place < 2 * TILE_DEV)
        if near:
            taken = inside & (slot < count)
            place = place - TILE_DEV
        else:
            taken = jnp.logical_not(inside) & (slot < count)
            place = jnp.where(place < TILE_DEV, place, place - TILE_DEV) ^ swapped
        list_ref[size] = tile
        list_ref[spare + size] = place
        size = size + jnp.where(taken, 1, 0)
    for slot in range(GROUP):
        list_ref[size + slot] = TILE_DEV
        list_ref[spare + size + slot] = 0
    return size


def add_slots(size, list_ref, left_ref, right_ref, value_ref, acc_ref):
    spare = list_ref.shape[0] // 2
    dims = (((1,), (1,)), ((), ()))

    def one_group(group, carry):
        exponents, sums = [], []
        for slot in range(GROUP):
            tile = list_ref[GROUP * group + slot]
            other = list_ref[spare + GROUP * group + slot]
            source = jnp.minimum(tile, TILE_DEV - 1)
            for bead in range(BEAD_DEV):
                exponent = jnp.dot(
                    left_ref[source, bead], right_ref[other, bead], preferred_element_type=jnp.float32
                )
                exponents.append((tile, other, bead, exponent))
        for tile, other, bead, exponent in exponents:
            weight = jnp.exp2(exponent)
            high = weight.astype(jnp.bfloat16)
            low = (weight - high.astype(jnp.float32)).astype(jnp.bfloat16)
            value = value_ref[other, bead]
            total = lax.dot_general(
                jnp.concatenate([value, value], 1),
                jnp.concatenate([high, low], 1),
                dims,
                preferred_element_type=jnp.float32,
            )
            sums.append((tile, bead, total))
        for tile, bead, total in sums:
            acc_ref[tile, bead] += total
        return carry

    lax.fori_loop(0, lax.div(size + GROUP - 1, GROUP), one_group, 0)


def near_kernel(
    tiles, local_ref, other_ref, count_ref, own_ref, mom_ref, mass_ref,
    acc_ref, left_ref, rows_ref, speed_ref, right_ref, value_ref, list_ref,
):
    size = list_slots(True, tiles, local_ref, other_ref, count_ref, list_ref)
    by_bead(rows_ref, own_ref)
    own = rows_ref[...]
    prepare_left(own, left_ref)
    prepare_right(own, 0, right_ref, value_ref)
    acc_ref[...] = jnp.zeros_like(acc_ref)
    mass = mass_ref[...]
    inverse = 1.0 / mass
    by_bead(speed_ref, [mom_ref[axis] * inverse for axis in range(3)] + [jnp.broadcast_to(mass, (BEAD_DEV, ATOM_DEV))])
    add_slots(size, list_ref, left_ref, right_ref, value_ref, acc_ref)


def far_kernel(
    tiles, local_ref, other_ref, count_ref, own_ref, second_ref, first_ref, near_ref, left_ref, speed_ref,
    out_ref, rows_ref, right_ref, value_ref, acc_ref, list_ref,
):
    size = list_slots(False, tiles, local_ref, other_ref, count_ref, list_ref)
    by_bead(rows_ref.at[0], first_ref)
    by_bead(rows_ref.at[1], second_ref)
    prepare_right(rows_ref[0], 0, right_ref, value_ref)
    prepare_right(rows_ref[1], TILE_DEV, right_ref, value_ref)
    acc_ref[...] = near_ref[...]
    add_slots(size, list_ref, left_ref, right_ref, value_ref, acc_ref)

    own = own_ref[...]
    comp = component((ROWS, TILE))
    lane = lax.broadcasted_iota(jnp.int32, (ROWS, TILE), 1)
    for tile in range(TILE_DEV):
        lanes = slice(tile * TILE, (tile + 1) * TILE)
        speed = speed_ref[:, lanes]
        sums = []
        for bead in range(BEAD_DEV):
            s = acc_ref[tile, bead]
            s = s[0:4] + s[4:8] + s[8:12]
            sums.append(own[4 * bead : 4 * bead + 4, lanes] * s[3:4] - s)
        factor = 0.5 * time_step / width_sq * own[3:4, lanes] / speed[3:4]
        push = jnp.where(comp == 3, 0.0, jnp.concatenate(sums, 0) * factor)
        speed = speed + push
        place = jnp.where(comp == 3, speed, own[:, lanes])
        out_ref[2 * tile] = jnp.where(lane < HALF, place, pltpu.roll(speed, HALF, 1))
        out_ref[2 * tile + 1] = jnp.where(lane < HALF, pltpu.roll(place, HALF, 1), speed)


def mode_kernel(x_ref, same_ref, drift_ref, pull_ref, out_ref):
    rows = x_ref.shape[0] * x_ref.shape[1]
    beads = rows // 4
    x = x_ref[...].reshape(rows, TILE)
    swapped = pltpu.roll(x, HALF, 1)
    lane = lax.broadcasted_iota(jnp.int32, (rows, TILE), 1)
    dot = functools.partial(jnp.dot, precision=lax.Precision.HIGHEST, preferred_element_type=jnp.float32)
    moved = dot(same_ref[...], x) + jnp.where(
        lane < HALF, dot(drift_ref[...], swapped), dot(pull_ref[...], swapped)
    )
    comp = component((rows, TILE))
    mass = x[3:4, :]
    step = jnp.where(comp == 3, 0.0, moved - pltpu.roll(moved, rows - 4, 0))
    spring = jnp.sum(step * step, axis=0, keepdims=True) * mass * (0.5 * omega_cycle * omega_cycle / beads)
    moved = jnp.where(lane < HALF, moved, moved * mass)
    out_ref[...] = jnp.where(comp == 3, spring, moved).reshape(out_ref.shape)


def unpack_kernel(y_ref, pos_ref, mom_ref, spring_ref):
    lane = lax.broadcasted_iota(jnp.int32, (BEAD_DEV, TILE), 1)
    for tile in range(TILE_DEV):
        lanes = slice(tile * TILE, (tile + 1) * TILE)
        for axis in range(4):
            rows = pl.ds(axis, BEAD_DEV, stride=4)
            first, second = y_ref[2 * tile, rows, :], y_ref[2 * tile + 1, rows, :]
            place = jnp.where(lane < HALF, first, pltpu.roll(second, HALF, 1))
            if axis == 3:
                spring_ref[:, lanes] = place[0:1]
            else:
                pos_ref[axis, :, lanes] = place
                mom_ref[axis, :, lanes] = jnp.where(lane < HALF, pltpu.roll(first, HALF, 1), second)


def f32(*shape):
    return jax.ShapeDtypeStruct(shape, jnp.float32)


def bf16(*shape):
    return jax.ShapeDtypeStruct(shape, jnp.bfloat16)


def pack(positions, charge):
    axis = lax.broadcasted_iota(jnp.int32, (4, BEAD_DEV, ATOM_DEV), 0)
    return jnp.where(axis < 3, jnp.pad(positions, ((0, 1), (0, 0), (0, 0))), charge[None, None])


def right_scratch(tiles):
    return [
        pltpu.VMEM((tiles, BEAD_DEV, 32, TILE), jnp.bfloat16),
        pltpu.VMEM((tiles, BEAD_DEV, 16, TILE), jnp.bfloat16),
    ]


def slot_scratch(plan):
    return [pltpu.SMEM((2 * (plan[0].shape[0] + GROUP),), jnp.int32)]


def near_forces(plan, own, momenta, masses, tiles):
    return pl.pallas_call(
        functools.partial(near_kernel, tiles),
        out_shape=(
            f32(TILE_DEV + 1, BEAD_DEV, 16, TILE),
            bf16(TILE_DEV, BEAD_DEV, TILE, 32),
            f32(ROWS, ATOM_DEV),
            f32(ROWS, ATOM_DEV),
        ),
        in_specs=[SMEM] * 3 + [VMEM] * 3,
        out_specs=(VMEM,) * 4,
        scratch_shapes=right_scratch(TILE_DEV) + slot_scratch(plan),
        compiler_params=PARAMS,
    )(*plan, own, momenta, masses[None])


def far_forces(plan, first, second, near, left, rows, speed, tiles, peers):
    return pl.pallas_call(
        functools.partial(far_kernel, tiles),
        out_shape=f32(peers, ROWS, TILE),
        in_specs=[SMEM] * 3 + [VMEM] * 6,
        out_specs=VMEM,
        scratch_shapes=[pltpu.VMEM((2, ROWS, ATOM_DEV), jnp.float32)]
        + right_scratch(2 * TILE_DEV)
        + [pltpu.VMEM((TILE_DEV + 1, BEAD_DEV, 16, TILE), jnp.float32)]
        + slot_scratch(plan),
        compiler_params=PARAMS,
    )(*plan, rows, second, first, near, left, speed)


def propagate(x, tables):
    return pl.pallas_call(
        mode_kernel, out_shape=f32(*x.shape), in_specs=[VMEM] * 4, out_specs=VMEM, compiler_params=PARAMS
    )(x, *tables)


def unpack(y):
    return pl.pallas_call(
        unpack_kernel,
        out_shape=(f32(3, BEAD_DEV, ATOM_DEV), f32(3, BEAD_DEV, ATOM_DEV), f32(1, ATOM_DEV)),
        in_specs=[VMEM],
        out_specs=(VMEM,) * 3,
        compiler_params=PARAMS,
    )(y)


def by_component(x):
    return jnp.transpose(x, (1, 0, 2))


def on_device(positions, momenta, charge, masses, pair_local, pair_other, pair_count):
    blocks = lax.axis_size("atom")
    peers = lax.axis_size("bead")
    own = pack(by_component(positions), charge)
    second = lax.ppermute(own, "atom", [(i, (i + 1 if i % 2 else i - 1) % blocks) for i in range(blocks)])
    first = lax.ppermute(own, "atom", [(i, i ^ 1) for i in range(blocks)])
    plan = (pair_local, pair_other, pair_count)
    tiles = TILE_DEV * blocks
    near, left, rows, speed = near_forces(plan, own, by_component(momenta), masses, tiles)
    sent = far_forces(plan, first, second, near, left, rows, speed, tiles, peers)
    x = lax.all_to_all(sent, "bead", 0, 0, tiled=True)
    y = propagate(x, [jnp.asarray(t) for t in bead_tables(BEAD_DEV * peers)])
    y = lax.all_to_all(y, "bead", 0, 0, tiled=True)
    new_positions, new_momenta, spring = unpack(y)
    return by_component(new_positions), by_component(new_momenta), spring[0]


def solution(mesh):
    return jax.shard_map(
        on_device,
        mesh=mesh,
        in_specs=(
            P("bead", None, "atom"),
            P("bead", None, "atom"),
            P("atom"),
            P("atom"),
            P("atom"),
            P("atom"),
            P("atom"),
        ),
        out_specs=(P("bead", None, "atom"), P("bead", None, "atom"), P("atom")),
        check_vma=False,
    )
```

profile of v0, /device:TPU:1, one launch (start us, length us, event | category | flops | bytes accessed | tf_op | source)
XLA Modules:
  0.0 47.1 jit_solution(13673813674291793940)
XLA Ops:
  0.6 0.0 copy-start.3
  0.7 0.9 %pad_select_fusion.own_ref = f32[4,4,1024]{2,1,0:T(4,128)S(1)} fusion(f32[3,4,1024]{2,1,0:T(4,128)} %bitcast.8, f32[1024]{0:T(1024)} %param.12, pred[4]{0:T(512)(128)(4,1)S(1)} %iota_compare_fusion), kind=kLoop, calls=%fused_computation | loop fusion | flops 16384 | bytes 118788 | tf_op jit(solution)/shard_map/jit(_where)/select_n | solution.py:266
  1.5 0.0 copy-start.4
  1.6 2.2 %collective-permute-start.1 = (f32[4,4,1024]{2,1,0:T(4,128)S(1)}, f32[4,4,1024]{2,1,0:T(4,128)S(1)}, u32[]{:S(2)}, u32[]{:S(2)}) collective-permute-start(f32[4,4,1024]{2,1,0:T(4,128)S(1)} %pad_select_fusion.own_ref), channel_id=1, source_target_pairs={{0,1},{1,0},{2,3},{3,2},{4,5},{5,4},{6,7},{7,6},{8,9},{9,8},{10,11... | collective-permute-start | bytes 196616 | tf_op jit(solution)/shard_map/ppermute | solution.py:335
  3.8 4.1 %collective-permute-start = (f32[4,4,1024]{2,1,0:T(4,128)S(1)}, f32[4,4,1024]{2,1,0:T(4,128)S(1)}, u32[]{:S(2)}, u32[]{:S(2)}) collective-permute-start(f32[4,4,1024]{2,1,0:T(4,128)S(1)} %pad_select_fusion.own_ref), channel_id=1, source_target_pairs={{0,15},{1,2},{2,1},{3,4},{4,3},{5,6},{6,5},{7,8},{8,7},{9,10},{10,... | collective-permute-start | bytes 196616 | tf_op jit(solution)/shard_map/ppermute | solution.py:334
  8.5 0.0 copy-start.5
  8.5 0.0 copy-start.6
  8.5 0.0 copy-done.3
  8.6 0.0 copy-done.4
  8.6 0.6 %copy-done.5 = s32[32]{0:T(128)S(1)} copy-done((s32[32]{0:T(128)S(1)}, s32[32]{0:T(128)}, u32[]{:S(2)}) %copy-start.5) | copy-done | bytes 152
  9.2 0.0 copy-done.6
  9.2 2.9 %shard_map.121 = (f32[9,4,16,128]{3,2,1,0:T(8,128)S(1)}, bf16[8,4,128,32]{3,2,1,0:T(8,128)(2,1)S(1)}, f32[16,1024]{1,0:T(8,128)S(1)}, f32[16,1024]{1,0:T(8,128)S(1)}) custom-call(s32[32]{0:T(128)S(1)} %copy-done.5, s32[32]{0:T(128)S(1)} %copy-done.6, s32[1]{0:T(128)S(6)} %copy.13.count_ref, f32[4,4,1024]{2,1,0:T(4,128)S(1)} %pad_select_fusion.own_ref, ...), custom_call_target="tpu_custom_call" | custom-call | tf_op jit(solution)/shard_map/pallas_call | solution.py:281
  12.1 0.0 collective-permute-done.1.first_ref
  12.1 0.0 collective-permute-done.second_ref
  12.2 0.0 copy-start.1
  12.2 0.0 copy-start.2
  12.2 2.8 %shard_map.122 = f32[16,16,128]{2,1,0:T(8,128)S(1)} custom-call(s32[32]{0:T(128)S(1)} %copy-done.5, s32[32]{0:T(128)S(1)} %copy-done.6, s32[1]{0:T(128)S(6)} %copy.13.count_ref, f32[16,1024]{1,0:T(8,128)S(1)} %get-tuple-element.10.own_ref, f32[4,4,1024]{2,1,0:T(4,128)S(1)} %collective-permute-done.second_ref, ...), custom_call_target="tpu_custom_call" | custom-call | tf_op jit(solution)/shard_map/pallas_call | solution.py:297
  15.0 0.0 copy-start
  15.0 18.8 %all_to_all.10.x_ref = f32[16,16,128]{2,1,0:T(8,128)S(1)} all-to-all(f32[16,16,128]{2,1,0:T(8,128)S(1)} %shard_map.122), channel_id=1, replica_groups=mesh['bead'=16,'atom'=16] {'bead'}, dimensions={0} | all-to-all | bytes 262144 | tf_op jit(solution)/shard_map/all_to_all | solution.py:340
  33.8 0.0 copy-done.1
  33.8 0.0 copy-done.2
  33.9 0.0 copy-done
  33.9 0.9 %shard_map.123 = f32[16,16,128]{2,1,0:T(8,128)S(1)} custom-call(f32[16,16,128]{2,1,0:T(8,128)S(1)} %all_to_all.10.x_ref, f32[256,256]{1,0:T(8,128)S(1)} %copy-done.2, f32[256,256]{1,0:T(8,128)S(1)} %copy-done.1, f32[256,256]{1,0:T(8,128)S(1)} %copy-done), custom_call_target="tpu_custom_call" | custom-call | tf_op jit(solution)/shard_map/pallas_call | solution.py:311
  34.8 11.6 %all_to_all.11.y_ref = f32[16,16,128]{2,1,0:T(8,128)S(1)} all-to-all(f32[16,16,128]{2,1,0:T(8,128)S(1)} %shard_map.123), channel_id=1, replica_groups=mesh['bead'=16,'atom'=16] {'bead'}, dimensions={0} | all-to-all | bytes 262144 | tf_op jit(solution)/shard_map/all_to_all | solution.py:342
  46.3 0.8 %shard_map.124 = (f32[3,4,1024]{2,1,0:T(4,128)}, f32[3,4,1024]{2,1,0:T(4,128)}, f32[1,1024]{1,0:T(1,128)}) custom-call(f32[16,16,128]{2,1,0:T(8,128)S(1)} %all_to_all.11.y_ref), custom_call_target="tpu_custom_call" | custom-call | tf_op jit(solution)/shard_map/pallas_call | solution.py:317
  (1 shorter events, 0.0 us)
Async XLA Ops:
  0.6 7.9 %copy-start.3 = (f32[4,3,1024]{2,0,1:T(4,128)S(1)}, f32[4,3,1024]{2,0,1:T(4,128)}, u32[]{:S(2)}) copy-start(f32[4,3,1024]{2,0,1:T(4,128)} %param.11) | copy-start | bytes 147460
  1.5 7.0 %copy-start.4 = (f32[1024]{0:T(1024)S(1)}, f32[1024]{0:T(1024)}, u32[]{:S(2)}) copy-start(f32[1024]{0:T(1024)} %param.13) | copy-start | bytes 12292
  1.6 10.6 %collective-permute-start.1 = (f32[4,4,1024]{2,1,0:T(4,128)S(1)}, f32[4,4,1024]{2,1,0:T(4,128)S(1)}, u32[]{:S(2)}, u32[]{:S(2)}) collective-permute-start(f32[4,4,1024]{2,1,0:T(4,128)S(1)} %pad_select_fusion.own_ref), channel_id=1, source_target_pairs={{0,1},{1,0},{2,3},{3,2},{4,5},{5,4},{6,7},{7,6},{8,9},{9,8},{10,11... | collective-permute-start | bytes 196616 | tf_op jit(solution)/shard_map/ppermute | solution.py:335
  3.8 8.4 %collective-permute-start = (f32[4,4,1024]{2,1,0:T(4,128)S(1)}, f32[4,4,1024]{2,1,0:T(4,128)S(1)}, u32[]{:S(2)}, u32[]{:S(2)}) collective-permute-start(f32[4,4,1024]{2,1,0:T(4,128)S(1)} %pad_select_fusion.own_ref), channel_id=1, source_target_pairs={{0,15},{1,2},{2,1},{3,4},{4,3},{5,6},{6,5},{7,8},{8,7},{9,10},{10,... | collective-permute-start | bytes 196616 | tf_op jit(solution)/shard_map/ppermute | solution.py:334
  8.5 0.7 %copy-start.5 = (s32[32]{0:T(128)S(1)}, s32[32]{0:T(128)}, u32[]{:S(2)}) copy-start(s32[32]{0:T(128)} %local_ref.3) | copy-start | bytes 388
  8.5 0.7 %copy-start.6 = (s32[32]{0:T(128)S(1)}, s32[32]{0:T(128)}, u32[]{:S(2)}) copy-start(s32[32]{0:T(128)} %other_ref.3) | copy-start | bytes 388
  12.2 21.7 %copy-start.1 = (f32[256,256]{1,0:T(8,128)S(1)}, f32[256,256]{1,0:T(8,128)}, u32[]{:S(2)}) copy-start(f32[256,256]{1,0:T(8,128)} %constant.12.clone.drift_ref) | copy-start | bytes 786436
  12.2 21.7 %copy-start.2 = (f32[256,256]{1,0:T(8,128)S(1)}, f32[256,256]{1,0:T(8,128)}, u32[]{:S(2)}) copy-start(f32[256,256]{1,0:T(8,128)} %constant.11.clone.same_ref) | copy-start | bytes 786436
  15.0 18.8 %copy-start = (f32[256,256]{1,0:T(8,128)S(1)}, f32[256,256]{1,0:T(8,128)}, u32[]{:S(2)}) copy-start(f32[256,256]{1,0:T(8,128)} %constant.13.clone.pull_ref) | copy-start | bytes 786436
where the time goes:
time: 47.8 us; the launch traced here: 47.1 us
  blocking collectives  30.4 us (64%)
  Pallas kernels  7.41 us (16%)
  starting transfers between devices  6.31 us (13%)
  between operations  1.39 us (3%)
  other arithmetic  0.9 us (2%)
  local copies, waits for them, and re-layouts  0.67 us (1%)
    all_to_all x1, blocking collectives, on_device(): x = lax.all_to_all(sent, 'bead', 0, 0, tiled=True)  18.8 us
    all_to_all x1, blocking collectives, on_device(): y = lax.all_to_all(y, 'bead', 0, 0, tiled=True)  11.6 us
    ppermute x1, starting transfers between devices, on_device(): lax.ppermute(own, 'atom', [(i, (i + 1 if i % 2 else i - 1) % blocks) for...  4.1 us
    pallas_call x1, Pallas kernels, near_forces(): pl.pallas_call(functools.partial(near_kernel, tiles), out_shape=(f32(TILE...  2.93 us
    pallas_call x1, Pallas kernels, far_forces(): pl.pallas_call(functools.partial(far_kernel, tiles), out_shape=f32(peers,...  2.83 us
    ppermute x1, starting transfers between devices, on_device(): first = lax.ppermute(own, 'atom', [(i, i ^ 1) for i in range(blocks)])  2.21 us
  transfers between devices with their start and end apart: 2, of which 0 were waited for; matrix products, arithmetic and copies ran while one was open for 0% of the time, Pallas kernels for 6%

commit v1 on v0

--- a/solution.py
+++ b/solution.py
@@ -20,10 +20,11 @@
 ROWS = 4 * BEAD_DEV
 HALF = TILE // 2
 GROUP = 8
+TAIL = 4
 SCALE = math.log2(math.e) / (2.0 * width_sq)
 
 VMEM = pl.BlockSpec(memory_space=pltpu.VMEM)
-SMEM = pl.BlockSpec(memory_space=pltpu.SMEM)
+ANY = pl.BlockSpec(memory_space=pl.ANY)
 PARAMS = pltpu.CompilerParams(vmem_limit_bytes=24 * 2**20)
 
 
@@ -114,6 +115,10 @@
             left_ref[tile, bead] = left[:, lanes].T.astype(jnp.bfloat16)
 
 
+def fetches(refs, plan_refs, sems):
+    return [pltpu.make_async_copy(ref, plan, sems.at[i]) for i, (ref, plan) in enumerate(zip(refs, plan_refs))]
+
+
 def list_slots(near, tiles, local_ref, other_ref, count_ref, list_ref):
     slots = local_ref.shape[0]
     spare = list_ref.shape[0] // 2
@@ -143,11 +148,11 @@
     spare = list_ref.shape[0] // 2
     dims = (((1,), (1,)), ((), ()))
 
-    def one_group(group, carry):
+    def one_group(start, slots):
         exponents, sums = [], []
-        for slot in range(GROUP):
-            tile = list_ref[GROUP * group + slot]
-            other = list_ref[spare + GROUP * group + slot]
+        for slot in range(slots):
+            tile = list_ref[start + slot]
+            other = list_ref[spare + start + slot]
             source = jnp.minimum(tile, TILE_DEV - 1)
             for bead in range(BEAD_DEV):
                 exponent = jnp.dot(
@@ -168,16 +173,27 @@
             sums.append((tile, bead, total))
         for tile, bead, total in sums:
             acc_ref[tile, bead] += total
+
+    groups = lax.div(size + GROUP - TAIL - 1, GROUP)
+
+    def whole(group, carry):
+        one_group(GROUP * group, GROUP)
         return carry
 
-    lax.fori_loop(0, lax.div(size + GROUP - 1, GROUP), one_group, 0)
+    lax.fori_loop(0, groups, whole, 0)
+
+    @pl.when(size > GROUP * groups)
+    def _():
+        one_group(GROUP * groups, TAIL)
 
 
 def near_kernel(
     tiles, local_ref, other_ref, count_ref, own_ref, mom_ref, mass_ref,
-    acc_ref, left_ref, rows_ref, speed_ref, right_ref, value_ref, list_ref,
+    acc_ref, left_ref, rows_ref, speed_ref, right_ref, value_ref, list_ref, *plan_refs,
 ):
-    size = list_slots(True, tiles, local_ref, other_ref, count_ref, list_ref)
+    copies = fetches((local_ref, other_ref, count_ref), plan_refs[:3], plan_refs[3])
+    for copy in copies:
+        copy.start()
     by_bead(rows_ref, own_ref)
     own = rows_ref[...]
     prepare_left(own, left_ref)
@@ -186,19 +202,27 @@
     mass = mass_ref[...]
     inverse = 1.0 / mass
     by_bead(speed_ref, [mom_ref[axis] * inverse for axis in range(3)] + [jnp.broadcast_to(mass, (BEAD_DEV, ATOM_DEV))])
+    for copy in copies:
+        copy.wait()
+    size = list_slots(True, tiles, *plan_refs[:3], list_ref)
     add_slots(size, list_ref, left_ref, right_ref, value_ref, acc_ref)
 
 
 def far_kernel(
     tiles, local_ref, other_ref, count_ref, own_ref, second_ref, first_ref, near_ref, left_ref, speed_ref,
-    out_ref, rows_ref, right_ref, value_ref, acc_ref, list_ref,
+    out_ref, rows_ref, right_ref, value_ref, acc_ref, list_ref, *plan_refs,
 ):
-    size = list_slots(False, tiles, local_ref, other_ref, count_ref, list_ref)
+    copies = fetches((local_ref, other_ref, count_ref), plan_refs[:3], plan_refs[3])
+    for copy in copies:
+        copy.start()
     by_bead(rows_ref.at[0], first_ref)
     by_bead(rows_ref.at[1], second_ref)
     prepare_right(rows_ref[0], 0, right_ref, value_ref)
     prepare_right(rows_ref[1], TILE_DEV, right_ref, value_ref)
     acc_ref[...] = near_ref[...]
+    for copy in copies:
+        copy.wait()
+    size = list_slots(False, tiles, *plan_refs[:3], list_ref)
     add_slots(size, list_ref, left_ref, right_ref, value_ref, acc_ref)
 
     own = own_ref[...]
@@ -274,7 +298,11 @@
 
 
 def slot_scratch(plan):
-    return [pltpu.SMEM((2 * (plan[0].shape[0] + GROUP),), jnp.int32)]
+    return (
+        [pltpu.SMEM((2 * (plan[0].shape[0] + GROUP),), jnp.int32)]
+        + [pltpu.SMEM(part.shape, jnp.int32) for part in plan]
+        + [pltpu.SemaphoreType.DMA((3,))]
+    )
 
 
 def near_forces(plan, own, momenta, masses, tiles):
@@ -286,7 +314,7 @@
             f32(ROWS, ATOM_DEV),
             f32(ROWS, ATOM_DEV),
         ),
-        in_specs=[SMEM] * 3 + [VMEM] * 3,
+        in_specs=[ANY] * 3 + [VMEM] * 3,
         out_specs=(VMEM,) * 4,
         scratch_shapes=right_scratch(TILE_DEV) + slot_scratch(plan),
         compiler_params=PARAMS,
@@ -297,7 +325,7 @@
     return pl.pallas_call(
         functools.partial(far_kernel, tiles),
         out_shape=f32(peers, ROWS, TILE),
-        in_specs=[SMEM] * 3 + [VMEM] * 6,
+        in_specs=[ANY] * 3 + [VMEM] * 6,
         out_specs=VMEM,
         scratch_shapes=[pltpu.VMEM((2, ROWS, ATOM_DEV), jnp.float32)]
         + right_scratch(2 * TILE_DEV)

time: 47.8 us -> 44.9 us (0.939)
  Pallas kernels: 7.41 us -> 3.71 us
  blocking collectives: 30.4 us -> 31.1 us
    pallas_call x1, Pallas kernels: 2.83 us -> 0.92 us  [far_forces(): pl.pallas_call(functools.partial(far_kernel, tiles), out_shape=f32(peers,...]
    pallas_call x1, Pallas kernels: 2.93 us -> 1.15 us  [near_forces(): pl.pallas_call(functools.partial(near_kernel, tiles), out_shape=(f32(TILE...]
    all_to_all x1, blocking collectives: 18.8 us -> 19.5 us  [on_device(): x = lax.all_to_all(sent, 'bead', 0, 0, tiled=True)]
  transfers between devices with their start and end apart: 2 -> 2, of which waited for: 0 -> 0; matrix products, arithmetic and copies ran while one was open for 0% -> 0% of each run, Pallas kernels for 6% -> 3%
where the time goes in v1:
time: 44.9 us; the launch traced here: 44.1 us
  blocking collectives  31.1 us (69%)
  starting transfers between devices  6.31 us (14%)
  Pallas kernels  3.71 us (8%)
  between operations  1.41 us (3%)
  other arithmetic  0.9 us (2%)
  local copies, waits for them, and re-layouts  0.67 us (1%)
    all_to_all x1, blocking collectives, on_device(): x = lax.all_to_all(sent, 'bead', 0, 0, tiled=True)  19.5 us
    all_to_all x1, blocking collectives, on_device(): y = lax.all_to_all(y, 'bead', 0, 0, tiled=True)  11.6 us
    ppermute x1, starting transfers between devices, on_device(): lax.ppermute(own, 'atom', [(i, (i + 1 if i % 2 else i - 1) % blocks) for...  4.1 us
    ppermute x1, starting transfers between devices, on_device(): first = lax.ppermute(own, 'atom', [(i, i ^ 1) for i in range(blocks)])  2.21 us
    pallas_call x1, Pallas kernels, near_forces(): pl.pallas_call(functools.partial(near_kernel, tiles), out_shape=(f32(TILE...  1.15 us
    pallas_call x1, Pallas kernels, far_forces(): pl.pallas_call(functools.partial(far_kernel, tiles), out_shape=f32(peers,...  0.92 us
  transfers between devices with their start and end apart: 2, of which 0 were waited for; matrix products, arithmetic and copies ran while one was open for 0% of the time, Pallas kernels for 3%

profile of v1, /device:TPU:1, one launch (start us, length us, event | category | flops | bytes accessed | tf_op | source)
XLA Modules:
  0.0 44.1 jit_solution(1097917060899712359)
XLA Ops:
  0.6 0.0 copy-start.3
  0.7 0.9 %pad_select_fusion.own_ref = f32[4,4,1024]{2,1,0:T(4,128)S(1)} fusion(f32[3,4,1024]{2,1,0:T(4,128)} %bitcast.8, f32[1024]{0:T(1024)} %param.12, pred[4]{0:T(512)(128)(4,1)S(1)} %iota_compare_fusion), kind=kLoop, calls=%fused_computation | loop fusion | flops 16384 | bytes 118788 | tf_op jit(solution)/shard_map/jit(_where)/select_n | solution.py:290
  1.5 0.0 copy-start.4
  1.6 2.2 %collective-permute-start.1 = (f32[4,4,1024]{2,1,0:T(4,128)S(1)}, f32[4,4,1024]{2,1,0:T(4,128)S(1)}, u32[]{:S(2)}, u32[]{:S(2)}) collective-permute-start(f32[4,4,1024]{2,1,0:T(4,128)S(1)} %pad_select_fusion.own_ref), channel_id=1, source_target_pairs={{0,1},{1,0},{2,3},{3,2},{4,5},{5,4},{6,7},{7,6},{8,9},{9,8},{10,11... | collective-permute-start | bytes 196616 | tf_op jit(solution)/shard_map/ppermute | solution.py:363
  3.8 4.1 %collective-permute-start = (f32[4,4,1024]{2,1,0:T(4,128)S(1)}, f32[4,4,1024]{2,1,0:T(4,128)S(1)}, u32[]{:S(2)}, u32[]{:S(2)}) collective-permute-start(f32[4,4,1024]{2,1,0:T(4,128)S(1)} %pad_select_fusion.own_ref), channel_id=1, source_target_pairs={{0,15},{1,2},{2,1},{3,4},{4,3},{5,6},{6,5},{7,8},{8,7},{9,10},{10,... | collective-permute-start | bytes 196616 | tf_op jit(solution)/shard_map/ppermute | solution.py:362
  8.5 0.0 copy-start.5
  8.5 0.0 copy-start.6
  8.5 0.0 copy-done.3
  8.6 0.0 copy-done.4
  8.6 0.6 %copy-done.5 = s32[32]{0:T(128)S(1)} copy-done((s32[32]{0:T(128)S(1)}, s32[32]{0:T(128)}, u32[]{:S(2)}) %copy-start.5) | copy-done | bytes 152
  9.2 0.0 copy-done.6
  9.2 1.1 %shard_map.121 = (f32[9,4,16,128]{3,2,1,0:T(8,128)S(1)}, bf16[8,4,128,32]{3,2,1,0:T(8,128)(2,1)S(1)}, f32[16,1024]{1,0:T(8,128)S(1)}, f32[16,1024]{1,0:T(8,128)S(1)}) custom-call(s32[32]{0:T(128)S(1)} %copy-done.5, s32[32]{0:T(128)S(1)} %copy-done.6, s32[1]{0:T(128)S(6)} %copy.13.count_ref, f32[4,4,1024]{2,1,0:T(4,128)S(1)} %pad_select_fusion.own_ref, ...), custom_call_target="tpu_custom_call" | custom-call | tf_op jit(solution)/shard_map/pallas_call | solution.py:309
  10.3 0.0 collective-permute-done.1.first_ref
  10.4 0.0 collective-permute-done.second_ref
  10.4 0.0 copy-start.1
  10.4 0.0 copy-start.2
  10.4 0.9 %shard_map.122 = f32[16,16,128]{2,1,0:T(8,128)S(1)} custom-call(s32[32]{0:T(128)S(1)} %copy-done.5, s32[32]{0:T(128)S(1)} %copy-done.6, s32[1]{0:T(128)S(6)} %copy.13.count_ref, f32[16,1024]{1,0:T(8,128)S(1)} %get-tuple-element.10.own_ref, f32[4,4,1024]{2,1,0:T(4,128)S(1)} %collective-permute-done.second_ref, ...), custom_call_target="tpu_custom_call" | custom-call | tf_op jit(solution)/shard_map/pallas_call | solution.py:325
  11.3 0.0 copy-start
  11.3 19.5 %all_to_all.10.x_ref = f32[16,16,128]{2,1,0:T(8,128)S(1)} all-to-all(f32[16,16,128]{2,1,0:T(8,128)S(1)} %shard_map.122), channel_id=1, replica_groups=mesh['bead'=16,'atom'=16] {'bead'}, dimensions={0} | all-to-all | bytes 262144 | tf_op jit(solution)/shard_map/all_to_all | solution.py:368
  30.8 0.0 copy-done.1
  30.8 0.0 copy-done.2
  30.8 0.0 copy-done
  30.8 0.9 %shard_map.123 = f32[16,16,128]{2,1,0:T(8,128)S(1)} custom-call(f32[16,16,128]{2,1,0:T(8,128)S(1)} %all_to_all.10.x_ref, f32[256,256]{1,0:T(8,128)S(1)} %copy-done.2, f32[256,256]{1,0:T(8,128)S(1)} %copy-done.1, f32[256,256]{1,0:T(8,128)S(1)} %copy-done), custom_call_target="tpu_custom_call" | custom-call | tf_op jit(solution)/shard_map/pallas_call | solution.py:339
  31.7 11.6 %all_to_all.11.y_ref = f32[16,16,128]{2,1,0:T(8,128)S(1)} all-to-all(f32[16,16,128]{2,1,0:T(8,128)S(1)} %shard_map.123), channel_id=1, replica_groups=mesh['bead'=16,'atom'=16] {'bead'}, dimensions={0} | all-to-all | bytes 262144 | tf_op jit(solution)/shard_map/all_to_all | solution.py:370
  43.3 0.8 %shard_map.124 = (f32[3,4,1024]{2,1,0:T(4,128)}, f32[3,4,1024]{2,1,0:T(4,128)}, f32[1,1024]{1,0:T(1,128)}) custom-call(f32[16,16,128]{2,1,0:T(8,128)S(1)} %all_to_all.11.y_ref), custom_call_target="tpu_custom_call" | custom-call | tf_op jit(solution)/shard_map/pallas_call | solution.py:345
  (1 shorter events, 0.0 us)
Async XLA Ops:
  0.6 7.9 %copy-start.3 = (f32[4,3,1024]{2,0,1:T(4,128)S(1)}, f32[4,3,1024]{2,0,1:T(4,128)}, u32[]{:S(2)}) copy-start(f32[4,3,1024]{2,0,1:T(4,128)} %param.11) | copy-start | bytes 147460
  1.5 7.0 %copy-start.4 = (f32[1024]{0:T(1024)S(1)}, f32[1024]{0:T(1024)}, u32[]{:S(2)}) copy-start(f32[1024]{0:T(1024)} %param.13) | copy-start | bytes 12292
  1.6 8.8 %collective-permute-start.1 = (f32[4,4,1024]{2,1,0:T(4,128)S(1)}, f32[4,4,1024]{2,1,0:T(4,128)S(1)}, u32[]{:S(2)}, u32[]{:S(2)}) collective-permute-start(f32[4,4,1024]{2,1,0:T(4,128)S(1)} %pad_select_fusion.own_ref), channel_id=1, source_target_pairs={{0,1},{1,0},{2,3},{3,2},{4,5},{5,4},{6,7},{7,6},{8,9},{9,8},{10,11... | collective-permute-start | bytes 196616 | tf_op jit(solution)/shard_map/ppermute | solution.py:363
  3.8 6.6 %collective-permute-start = (f32[4,4,1024]{2,1,0:T(4,128)S(1)}, f32[4,4,1024]{2,1,0:T(4,128)S(1)}, u32[]{:S(2)}, u32[]{:S(2)}) collective-permute-start(f32[4,4,1024]{2,1,0:T(4,128)S(1)} %pad_select_fusion.own_ref), channel_id=1, source_target_pairs={{0,15},{1,2},{2,1},{3,4},{4,3},{5,6},{6,5},{7,8},{8,7},{9,10},{10,... | collective-permute-start | bytes 196616 | tf_op jit(solution)/shard_map/ppermute | solution.py:362
  8.5 0.7 %copy-start.5 = (s32[32]{0:T(128)S(1)}, s32[32]{0:T(128)}, u32[]{:S(2)}) copy-start(s32[32]{0:T(128)} %local_ref.3) | copy-start | bytes 388
  8.5 0.7 %copy-start.6 = (s32[32]{0:T(128)S(1)}, s32[32]{0:T(128)}, u32[]{:S(2)}) copy-start(s32[32]{0:T(128)} %other_ref.3) | copy-start | bytes 388
  10.4 20.5 %copy-start.1 = (f32[256,256]{1,0:T(8,128)S(1)}, f32[256,256]{1,0:T(8,128)}, u32[]{:S(2)}) copy-start(f32[256,256]{1,0:T(8,128)} %constant.12.clone.drift_ref) | copy-start | bytes 786436
  10.4 20.5 %copy-start.2 = (f32[256,256]{1,0:T(8,128)S(1)}, f32[256,256]{1,0:T(8,128)}, u32[]{:S(2)}) copy-start(f32[256,256]{1,0:T(8,128)} %constant.11.clone.same_ref) | copy-start | bytes 786436
  11.3 19.5 %copy-start = (f32[256,256]{1,0:T(8,128)S(1)}, f32[256,256]{1,0:T(8,128)}, u32[]{:S(2)}) copy-start(f32[256,256]{1,0:T(8,128)} %constant.13.clone.pull_ref) | copy-start | bytes 786436

commit v2 on v1

--- a/solution.py
+++ b/solution.py
@@ -24,7 +24,7 @@
 SCALE = math.log2(math.e) / (2.0 * width_sq)
 
 VMEM = pl.BlockSpec(memory_space=pltpu.VMEM)
-ANY = pl.BlockSpec(memory_space=pl.ANY)
+HBM = pl.BlockSpec(memory_space=pltpu.HBM)
 PARAMS = pltpu.CompilerParams(vmem_limit_bytes=24 * 2**20)
 
 
@@ -314,7 +314,7 @@
             f32(ROWS, ATOM_DEV),
             f32(ROWS, ATOM_DEV),
         ),
-        in_specs=[ANY] * 3 + [VMEM] * 3,
+        in_specs=[HBM] * 3 + [VMEM] * 3,
         out_specs=(VMEM,) * 4,
         scratch_shapes=right_scratch(TILE_DEV) + slot_scratch(plan),
         compiler_params=PARAMS,
@@ -325,7 +325,7 @@
     return pl.pallas_call(
         functools.partial(far_kernel, tiles),
         out_shape=f32(peers, ROWS, TILE),
-        in_specs=[ANY] * 3 + [VMEM] * 6,
+        in_specs=[HBM] * 3 + [VMEM] * 6,
         out_specs=VMEM,
         scratch_shapes=[pltpu.VMEM((2, ROWS, ATOM_DEV), jnp.float32)]
         + right_scratch(2 * TILE_DEV)
@@ -361,7 +361,8 @@
     own = pack(by_component(positions), charge)
     second = lax.ppermute(own, "atom", [(i, (i + 1 if i % 2 else i - 1) % blocks) for i in range(blocks)])
     first = lax.ppermute(own, "atom", [(i, i ^ 1) for i in range(blocks)])
-    plan = (pair_local, pair_other, pair_count)
+    plan = tuple(pltpu.with_memory_space_constraint(part, pltpu.HBM) for part in (pair_local, pair_other))
+    plan += (pair_count,)
     tiles = TILE_DEV * blocks
     near, left, rows, speed = near_forces(plan, own, by_component(momenta), masses, tiles)
     sent = far_forces(plan, first, second, near, left, rows, speed, tiles, peers)

time: 44.9 us -> 47.1 us (1.049); the launches traced: 44.1 us -> 47.3 us
  Pallas kernels: 3.71 us -> 8.26 us
  blocking collectives: 31.1 us -> 30.4 us
  local copies, waits for them, and re-layouts: 0.67 us -> 0.03 us
    pallas_call x1, Pallas kernels: 0.92 us -> 3.59 us  [far_forces(): pl.pallas_call(functools.partial(far_kernel, tiles), out_shape=f32(peers,...]
    pallas_call x1, Pallas kernels: 1.15 us -> 3.03 us  [near_forces(): pl.pallas_call(functools.partial(near_kernel, tiles), out_shape=(f32(TILE...]
    all_to_all x1, blocking collectives: 19.5 us -> 18.8 us  [on_device(): x = lax.all_to_all(sent, 'bead', 0, 0, tiled=True)]
    unnamed x14 -> x10, local copies, waits for them, and re-layouts: 0.67 us -> 0.03 us
  transfers between devices with their start and end apart: 2 -> 2, of which waited for: 0 -> 0; matrix products, arithmetic and copies ran while one was open for 0% -> 0% of each run, Pallas kernels for 3% -> 6%
where the time goes in v2:
time: 47.1 us; the launch traced here: 47.3 us
  blocking collectives  30.4 us (65%)
  Pallas kernels  8.26 us (18%)
  starting transfers between devices  6.31 us (13%)
  between operations  1.39 us (3%)
  other arithmetic  0.9 us (2%)
    all_to_all x1, blocking collectives, on_device(): x = lax.all_to_all(sent, 'bead', 0, 0, tiled=True)  18.8 us
    all_to_all x1, blocking collectives, on_device(): y = lax.all_to_all(y, 'bead', 0, 0, tiled=True)  11.6 us
    ppermute x1, starting transfers between devices, on_device(): lax.ppermute(own, 'atom', [(i, (i + 1 if i % 2 else i - 1) % blocks) for...  4.1 us
    pallas_call x1, Pallas kernels, far_forces(): pl.pallas_call(functools.partial(far_kernel, tiles), out_shape=f32(peers,...  3.59 us
    pallas_call x1, Pallas kernels, near_forces(): pl.pallas_call(functools.partial(near_kernel, tiles), out_shape=(f32(TILE...  3.03 us
    ppermute x1, starting transfers between devices, on_device(): first = lax.ppermute(own, 'atom', [(i, i ^ 1) for i in range(blocks)])  2.21 us
  transfers between devices with their start and end apart: 2, of which 0 were waited for; matrix products, arithmetic and copies ran while one was open for 0% of the time, Pallas kernels for 6%

profile of v2, /device:TPU:1, one launch (start us, length us, event | category | flops | bytes accessed | tf_op | source)
XLA Modules:
  0.0 47.3 jit_solution(14406414606932927760)
XLA Ops:
  0.6 0.0 copy-start.3
  0.7 0.9 %pad_select_fusion.own_ref = f32[4,4,1024]{2,1,0:T(4,128)S(1)} fusion(f32[3,4,1024]{2,1,0:T(4,128)} %bitcast.8, f32[1024]{0:T(1024)} %param.12, pred[4]{0:T(512)(128)(4,1)S(1)} %iota_compare_fusion), kind=kLoop, calls=%fused_computation | loop fusion | flops 16384 | bytes 118788 | tf_op jit(solution)/shard_map/jit(_where)/select_n | solution.py:290
  1.5 0.0 copy-start.4
  1.6 2.2 %collective-permute-start.1 = (f32[4,4,1024]{2,1,0:T(4,128)S(1)}, f32[4,4,1024]{2,1,0:T(4,128)S(1)}, u32[]{:S(2)}, u32[]{:S(2)}) collective-permute-start(f32[4,4,1024]{2,1,0:T(4,128)S(1)} %pad_select_fusion.own_ref), channel_id=1, source_target_pairs={{0,1},{1,0},{2,3},{3,2},{4,5},{5,4},{6,7},{7,6},{8,9},{9,8},{10,11... | collective-permute-start | bytes 196616 | tf_op jit(solution)/shard_map/ppermute | solution.py:363
  3.8 4.1 %collective-permute-start = (f32[4,4,1024]{2,1,0:T(4,128)S(1)}, f32[4,4,1024]{2,1,0:T(4,128)S(1)}, u32[]{:S(2)}, u32[]{:S(2)}) collective-permute-start(f32[4,4,1024]{2,1,0:T(4,128)S(1)} %pad_select_fusion.own_ref), channel_id=1, source_target_pairs={{0,15},{1,2},{2,1},{3,4},{4,3},{5,6},{6,5},{7,8},{8,7},{9,10},{10,... | collective-permute-start | bytes 196616 | tf_op jit(solution)/shard_map/ppermute | solution.py:362
  8.5 0.0 copy-done.3
  8.5 0.0 copy-done.4
  8.5 3.0 %shard_map.121 = (f32[9,4,16,128]{3,2,1,0:T(8,128)S(1)}, bf16[8,4,128,32]{3,2,1,0:T(8,128)(2,1)S(1)}, f32[16,1024]{1,0:T(8,128)S(1)}, f32[16,1024]{1,0:T(8,128)S(1)}) custom-call(s32[32]{0:T(128)} %local_ref.3, s32[32]{0:T(128)} %other_ref.3, s32[1]{0:T(128)S(6)} %copy.13.count_ref, f32[4,4,1024]{2,1,0:T(4,128)S(1)} %pad_select_fusion.own_ref, ...), custom_call_target="tpu_custom_call" | custom-call | tf_op jit(solution)/shard_map/pallas_call | solution.py:309
  11.6 0.0 collective-permute-done.1.first_ref
  11.6 0.0 collective-permute-done.second_ref
  11.6 0.0 copy-start.1
  11.6 0.0 copy-start.2
  11.6 3.6 %shard_map.122 = f32[16,16,128]{2,1,0:T(8,128)S(1)} custom-call(s32[32]{0:T(128)} %local_ref.3, s32[32]{0:T(128)} %other_ref.3, s32[1]{0:T(128)S(6)} %copy.13.count_ref, f32[16,1024]{1,0:T(8,128)S(1)} %get-tuple-element.10.own_ref, f32[4,4,1024]{2,1,0:T(4,128)S(1)} %collective-permute-done.second_ref, f32[4,4,1024]{2,1,0:T(4,128)S(1)} %collective-permute-done.1.first_ref, ...), custom_call_target="tpu_custom_call" | custom-call | tf_op jit(solution)/shard_map/pallas_call | solution.py:325
  15.2 0.0 copy-start
  15.2 18.8 %all_to_all.10.x_ref = f32[16,16,128]{2,1,0:T(8,128)S(1)} all-to-all(f32[16,16,128]{2,1,0:T(8,128)S(1)} %shard_map.122), channel_id=1, replica_groups=mesh['bead'=16,'atom'=16] {'bead'}, dimensions={0} | all-to-all | bytes 262144 | tf_op jit(solution)/shard_map/all_to_all | solution.py:369
  34.0 0.0 copy-done.1
  34.0 0.0 copy-done.2
  34.1 0.0 copy-done
  34.1 0.9 %shard_map.123 = f32[16,16,128]{2,1,0:T(8,128)S(1)} custom-call(f32[16,16,128]{2,1,0:T(8,128)S(1)} %all_to_all.10.x_ref, f32[256,256]{1,0:T(8,128)S(1)} %copy-done.2, f32[256,256]{1,0:T(8,128)S(1)} %copy-done.1, f32[256,256]{1,0:T(8,128)S(1)} %copy-done), custom_call_target="tpu_custom_call" | custom-call | tf_op jit(solution)/shard_map/pallas_call | solution.py:339
  34.9 11.6 %all_to_all.11.y_ref = f32[16,16,128]{2,1,0:T(8,128)S(1)} all-to-all(f32[16,16,128]{2,1,0:T(8,128)S(1)} %shard_map.123), channel_id=1, replica_groups=mesh['bead'=16,'atom'=16] {'bead'}, dimensions={0} | all-to-all | bytes 262144 | tf_op jit(solution)/shard_map/all_to_all | solution.py:371
  46.5 0.8 %shard_map.124 = (f32[3,4,1024]{2,1,0:T(4,128)}, f32[3,4,1024]{2,1,0:T(4,128)}, f32[1,1024]{1,0:T(1,128)}) custom-call(f32[16,16,128]{2,1,0:T(8,128)S(1)} %all_to_all.11.y_ref), custom_call_target="tpu_custom_call" | custom-call | tf_op jit(solution)/shard_map/pallas_call | solution.py:345
  (1 shorter events, 0.0 us)
Async XLA Ops:
  0.6 7.9 %copy-start.3 = (f32[4,3,1024]{2,0,1:T(4,128)S(1)}, f32[4,3,1024]{2,0,1:T(4,128)}, u32[]{:S(2)}) copy-start(f32[4,3,1024]{2,0,1:T(4,128)} %param.11) | copy-start | bytes 147460
  1.5 7.0 %copy-start.4 = (f32[1024]{0:T(1024)S(1)}, f32[1024]{0:T(1024)}, u32[]{:S(2)}) copy-start(f32[1024]{0:T(1024)} %param.13) | copy-start | bytes 12292
  1.6 10.0 %collective-permute-start.1 = (f32[4,4,1024]{2,1,0:T(4,128)S(1)}, f32[4,4,1024]{2,1,0:T(4,128)S(1)}, u32[]{:S(2)}, u32[]{:S(2)}) collective-permute-start(f32[4,4,1024]{2,1,0:T(4,128)S(1)} %pad_select_fusion.own_ref), channel_id=1, source_target_pairs={{0,1},{1,0},{2,3},{3,2},{4,5},{5,4},{6,7},{7,6},{8,9},{9,8},{10,11... | collective-permute-start | bytes 196616 | tf_op jit(solution)/shard_map/ppermute | solution.py:363
  3.8 7.8 %collective-permute-start = (f32[4,4,1024]{2,1,0:T(4,128)S(1)}, f32[4,4,1024]{2,1,0:T(4,128)S(1)}, u32[]{:S(2)}, u32[]{:S(2)}) collective-permute-start(f32[4,4,1024]{2,1,0:T(4,128)S(1)} %pad_select_fusion.own_ref), channel_id=1, source_target_pairs={{0,15},{1,2},{2,1},{3,4},{4,3},{5,6},{6,5},{7,8},{8,7},{9,10},{10,... | collective-permute-start | bytes 196616 | tf_op jit(solution)/shard_map/ppermute | solution.py:362
  11.6 22.4 %copy-start.1 = (f32[256,256]{1,0:T(8,128)S(1)}, f32[256,256]{1,0:T(8,128)}, u32[]{:S(2)}) copy-start(f32[256,256]{1,0:T(8,128)} %constant.12.clone.drift_ref) | copy-start | bytes 786436
  11.6 22.4 %copy-start.2 = (f32[256,256]{1,0:T(8,128)S(1)}, f32[256,256]{1,0:T(8,128)}, u32[]{:S(2)}) copy-start(f32[256,256]{1,0:T(8,128)} %constant.11.clone.same_ref) | copy-start | bytes 786436
  15.2 18.8 %copy-start = (f32[256,256]{1,0:T(8,128)S(1)}, f32[256,256]{1,0:T(8,128)}, u32[]{:S(2)}) copy-start(f32[256,256]{1,0:T(8,128)} %constant.13.clone.pull_ref) | copy-start | bytes 786436

commit v3 on v2

--- a/solution.py
+++ b/solution.py
@@ -3,6 +3,7 @@
 
 import jax
 import jax.numpy as jnp
+import ml_dtypes
 import numpy as np
 from jax import lax
 from jax.experimental import pallas as pl
@@ -25,6 +26,7 @@
 
 VMEM = pl.BlockSpec(memory_space=pltpu.VMEM)
 HBM = pl.BlockSpec(memory_space=pltpu.HBM)
+ANY = pl.BlockSpec(memory_space=pl.ANY)
 PARAMS = pltpu.CompilerParams(vmem_limit_bytes=24 * 2**20)
 
 
@@ -51,10 +53,12 @@
     reach = np.where(omega > 0, sine / np.where(omega > 0, omega, 1.0), time_step)
     parts = (np.cos(omega * time_step), reach, -omega * sine)
     used = np.diag([1.0, 1.0, 1.0, 0.0])
-    return [
-        np.kron((table * part[None, :]) @ table.T, used).astype(np.float32)
-        for part in parts
-    ]
+    rest = np.concatenate([np.kron((table * part[None, :]) @ table.T, used) for part in parts])
+    split = []
+    for _ in range(3):
+        split.append(rest.astype(ml_dtypes.bfloat16))
+        rest = rest - split[-1].astype(np.float64)
+    return split
 
 
 def component(shape):
@@ -189,10 +193,12 @@
 
 def near_kernel(
     tiles, local_ref, other_ref, count_ref, own_ref, mom_ref, mass_ref,
-    acc_ref, left_ref, rows_ref, speed_ref, right_ref, value_ref, list_ref, *plan_refs,
+    acc_ref, left_ref, rows_ref, speed_ref, passed_local_ref, passed_other_ref,
+    right_ref, value_ref, list_ref, *plan_refs,
 ):
     copies = fetches((local_ref, other_ref, count_ref), plan_refs[:3], plan_refs[3])
-    for copy in copies:
+    passed = fetches((local_ref, other_ref), (passed_local_ref, passed_other_ref), plan_refs[4])
+    for copy in copies + passed:
         copy.start()
     by_bead(rows_ref, own_ref)
     own = rows_ref[...]
@@ -206,6 +212,8 @@
         copy.wait()
     size = list_slots(True, tiles, *plan_refs[:3], list_ref)
     add_slots(size, list_ref, left_ref, right_ref, value_ref, acc_ref)
+    for copy in passed:
+        copy.wait()
 
 
 def far_kernel(
@@ -244,16 +252,18 @@
         out_ref[2 * tile + 1] = jnp.where(lane < HALF, pltpu.roll(place, HALF, 1), speed)
 
 
-def mode_kernel(x_ref, same_ref, drift_ref, pull_ref, out_ref):
+def mode_kernel(x_ref, high_ref, mid_ref, low_ref, out_ref):
     rows = x_ref.shape[0] * x_ref.shape[1]
     beads = rows // 4
     x = x_ref[...].reshape(rows, TILE)
-    swapped = pltpu.roll(x, HALF, 1)
+    high, mid, low = (part.astype(jnp.bfloat16) for part in split3(x))
+    both = jnp.concatenate([high, mid], 1)
+    dot = functools.partial(jnp.dot, preferred_element_type=jnp.float32)
+    wide = dot(high_ref[...], both) + dot(mid_ref[...], both)
+    total = wide[:, :TILE] + (wide[:, TILE:] + (dot(high_ref[...], low) + dot(low_ref[...], high)))
     lane = lax.broadcasted_iota(jnp.int32, (rows, TILE), 1)
-    dot = functools.partial(jnp.dot, precision=lax.Precision.HIGHEST, preferred_element_type=jnp.float32)
-    moved = dot(same_ref[...], x) + jnp.where(
-        lane < HALF, dot(drift_ref[...], swapped), dot(pull_ref[...], swapped)
-    )
+    crossed = jnp.where(lane < HALF, total[2 * rows :], total[rows : 2 * rows])
+    moved = total[:rows] + pltpu.roll(crossed, HALF, 1)
     comp = component((rows, TILE))
     mass = x[3:4, :]
     step = jnp.where(comp == 3, 0.0, moved - pltpu.roll(moved, rows - 4, 0))
@@ -313,10 +323,11 @@
             bf16(TILE_DEV, BEAD_DEV, TILE, 32),
             f32(ROWS, ATOM_DEV),
             f32(ROWS, ATOM_DEV),
+            *(jax.ShapeDtypeStruct(part.shape, part.dtype) for part in plan[:2]),
         ),
         in_specs=[HBM] * 3 + [VMEM] * 3,
-        out_specs=(VMEM,) * 4,
-        scratch_shapes=right_scratch(TILE_DEV) + slot_scratch(plan),
+        out_specs=(VMEM,) * 6,
+        scratch_shapes=right_scratch(TILE_DEV) + slot_scratch(plan) + [pltpu.SemaphoreType.DMA((2,))],
         compiler_params=PARAMS,
     )(*plan, own, momenta, masses[None])
 
@@ -325,7 +336,7 @@
     return pl.pallas_call(
         functools.partial(far_kernel, tiles),
         out_shape=f32(peers, ROWS, TILE),
-        in_specs=[HBM] * 3 + [VMEM] * 6,
+        in_specs=[VMEM] * 2 + [ANY] + [VMEM] * 6,
         out_specs=VMEM,
         scratch_shapes=[pltpu.VMEM((2, ROWS, ATOM_DEV), jnp.float32)]
         + right_scratch(2 * TILE_DEV)
@@ -364,10 +375,10 @@
     plan = tuple(pltpu.with_memory_space_constraint(part, pltpu.HBM) for part in (pair_local, pair_other))
     plan += (pair_count,)
     tiles = TILE_DEV * blocks
-    near, left, rows, speed = near_forces(plan, own, by_component(momenta), masses, tiles)
-    sent = far_forces(plan, first, second, near, left, rows, speed, tiles, peers)
+    near, left, rows, speed, *passed = near_forces(plan, own, by_component(momenta), masses, tiles)
+    sent = far_forces((*passed, pair_count), first, second, near, left, rows, speed, tiles, peers)
     x = lax.all_to_all(sent, "bead", 0, 0, tiled=True)
-    y = propagate(x, [jnp.asarray(t) for t in bead_tables(BEAD_DEV * peers)])
+    y = propagate(x, [jnp.asarray(part) for part in bead_tables(BEAD_DEV * peers)])
     y = lax.all_to_all(y, "bead", 0, 0, tiled=True)
     new_positions, new_momenta, spring = unpack(y)
     return by_component(new_positions), by_component(new_momenta), spring[0]

time: 47.1 us -> 45.2 us (0.960); the launches traced: 47.3 us -> 44.3 us
  Pallas kernels: 8.26 us -> 4.6 us
  blocking collectives: 30.4 us -> 31 us
    pallas_call x1, Pallas kernels: 3.59 us -> 1.46 us  [far_forces(): pl.pallas_call(functools.partial(far_kernel, tiles), out_shape=f32(peers,...]
    pallas_call x1, Pallas kernels: 3.03 us -> 1.71 us  [near_forces(): pl.pallas_call(functools.partial(near_kernel, tiles), out_shape=(f32(TILE...]
    all_to_all x1, blocking collectives: 18.8 us -> 19.4 us  [on_device(): x = lax.all_to_all(sent, 'bead', 0, 0, tiled=True)]
  transfers between devices with their start and end apart: 2 -> 2, of which waited for: 0 -> 0; matrix products, arithmetic and copies ran while one was open for 0% -> 0% of each run, Pallas kernels for 6% -> 4%
where the time goes in v3:
time: 45.2 us; the launch traced here: 44.3 us
  blocking collectives  31 us (69%)
  starting transfers between devices  6.31 us (14%)
  Pallas kernels  4.6 us (10%)
  between operations  1.39 us (3%)
  other arithmetic  0.9 us (2%)
    all_to_all x1, blocking collectives, on_device(): x = lax.all_to_all(sent, 'bead', 0, 0, tiled=True)  19.4 us
    all_to_all x1, blocking collectives, on_device(): y = lax.all_to_all(y, 'bead', 0, 0, tiled=True)  11.6 us
    ppermute x1, starting transfers between devices, on_device(): lax.ppermute(own, 'atom', [(i, (i + 1 if i % 2 else i - 1) % blocks) for...  4.1 us
    ppermute x1, starting transfers between devices, on_device(): first = lax.ppermute(own, 'atom', [(i, i ^ 1) for i in range(blocks)])  2.21 us
    pallas_call x1, Pallas kernels, near_forces(): pl.pallas_call(functools.partial(near_kernel, tiles), out_shape=(f32(TILE...  1.71 us
    pallas_call x1, Pallas kernels, far_forces(): pl.pallas_call(functools.partial(far_kernel, tiles), out_shape=f32(peers,...  1.46 us
  transfers between devices with their start and end apart: 2, of which 0 were waited for; matrix products, arithmetic and copies ran while one was open for 0% of the time, Pallas kernels for 4%

profile of v3, /device:TPU:1, one launch (start us, length us, event | category | flops | bytes accessed | tf_op | source)
XLA Modules:
  0.0 44.3 jit_solution(17641489403297019927)
XLA Ops:
  0.6 0.0 copy-start.3
  0.7 0.9 %pad_select_fusion.own_ref = f32[4,4,1024]{2,1,0:T(4,128)S(1)} fusion(f32[3,4,1024]{2,1,0:T(4,128)} %bitcast.8, f32[1024]{0:T(1024)} %param.12, pred[4]{0:T(512)(128)(4,1)S(1)} %iota_compare_fusion), kind=kLoop, calls=%fused_computation | loop fusion | flops 16384 | bytes 118788 | tf_op jit(solution)/shard_map/jit(_where)/select_n | solution.py:300
  1.5 0.0 copy-start.4
  1.6 2.2 %collective-permute-start.1 = (f32[4,4,1024]{2,1,0:T(4,128)S(1)}, f32[4,4,1024]{2,1,0:T(4,128)S(1)}, u32[]{:S(2)}, u32[]{:S(2)}) collective-permute-start(f32[4,4,1024]{2,1,0:T(4,128)S(1)} %pad_select_fusion.own_ref), channel_id=1, source_target_pairs={{0,1},{1,0},{2,3},{3,2},{4,5},{5,4},{6,7},{7,6},{8,9},{9,8},{10,11... | collective-permute-start | bytes 196616 | tf_op jit(solution)/shard_map/ppermute | solution.py:374
  3.8 4.1 %collective-permute-start = (f32[4,4,1024]{2,1,0:T(4,128)S(1)}, f32[4,4,1024]{2,1,0:T(4,128)S(1)}, u32[]{:S(2)}, u32[]{:S(2)}) collective-permute-start(f32[4,4,1024]{2,1,0:T(4,128)S(1)} %pad_select_fusion.own_ref), channel_id=1, source_target_pairs={{0,15},{1,2},{2,1},{3,4},{4,3},{5,6},{6,5},{7,8},{8,7},{9,10},{10,... | collective-permute-start | bytes 196616 | tf_op jit(solution)/shard_map/ppermute | solution.py:373
  8.5 0.0 copy-done.3
  8.5 0.0 copy-done.4
  8.5 1.7 %shard_map.121 = (f32[9,4,16,128]{3,2,1,0:T(8,128)S(1)}, bf16[8,4,128,32]{3,2,1,0:T(8,128)(2,1)S(1)}, f32[16,1024]{1,0:T(8,128)S(1)}, f32[16,1024]{1,0:T(8,128)S(1)}, s32[32]{0:T(128)S(1)}, /*index=5*/s32[32]{0:T(128)S(1)}) custom-call(s32[32]{0:T(128)} %local_ref.1, s32[32]{0:T(128)} %other_ref.1, s32[1]{0:T(128)S(6)} %copy.13.count_ref, ...), custom_call_target="tpu_custom_call" | custom-call | tf_op jit(solution)/shard_map/pallas_call | solution.py:319
  10.3 0.0 collective-permute-done.1.first_ref
  10.3 0.0 collective-permute-done.second_ref
  10.3 0.0 copy-start
  10.3 0.0 copy-start.1
  10.3 0.0 copy-start.2
  10.3 1.5 %shard_map.122 = f32[16,16,128]{2,1,0:T(8,128)S(1)} custom-call(s32[32]{0:T(128)S(1)} %get-tuple-element.12.local_ref, s32[32]{0:T(128)S(1)} %get-tuple-element.13.other_ref, s32[1]{0:T(128)S(6)} %copy.13.count_ref, f32[16,1024]{1,0:T(8,128)S(1)} %get-tuple-element.14.own_ref, f32[4,4,1024]{2,1,0:T(4,128)S(1)} %collective-permute-done.second_ref, ...), custom_call_target="tpu_custom_call" | custom-call | tf_op jit(solution)/shard_map/pallas_call | solution.py:336
  11.8 19.4 %all_to_all.10.x_ref = f32[16,16,128]{2,1,0:T(8,128)S(1)} all-to-all(f32[16,16,128]{2,1,0:T(8,128)S(1)} %shard_map.122), channel_id=1, replica_groups=mesh['bead'=16,'atom'=16] {'bead'}, dimensions={0} | all-to-all | bytes 262144 | tf_op jit(solution)/shard_map/all_to_all | solution.py:380
  31.2 0.0 copy-done
  31.2 0.0 copy-done.1
  31.2 0.0 copy-done.2
  31.2 0.7 %shard_map.123 = f32[16,16,128]{2,1,0:T(8,128)S(1)} custom-call(f32[16,16,128]{2,1,0:T(8,128)S(1)} %all_to_all.10.x_ref, bf16[768,256]{1,0:T(8,128)(2,1)S(1)} %copy-done.2, bf16[768,256]{1,0:T(8,128)(2,1)S(1)} %copy-done.1, bf16[768,256]{1,0:T(8,128)(2,1)S(1)} %copy-done), custom_call_target="tpu_custom_call" | custom-call | tf_op jit(solution)/shard_map/pallas_call | solution.py:350
  31.9 11.6 %all_to_all.11.y_ref = f32[16,16,128]{2,1,0:T(8,128)S(1)} all-to-all(f32[16,16,128]{2,1,0:T(8,128)S(1)} %shard_map.123), channel_id=1, replica_groups=mesh['bead'=16,'atom'=16] {'bead'}, dimensions={0} | all-to-all | bytes 262144 | tf_op jit(solution)/shard_map/all_to_all | solution.py:382
  43.5 0.8 %shard_map.124 = (f32[3,4,1024]{2,1,0:T(4,128)}, f32[3,4,1024]{2,1,0:T(4,128)}, f32[1,1024]{1,0:T(1,128)}) custom-call(f32[16,16,128]{2,1,0:T(8,128)S(1)} %all_to_all.11.y_ref), custom_call_target="tpu_custom_call" | custom-call | tf_op jit(solution)/shard_map/pallas_call | solution.py:356
  (1 shorter events, 0.0 us)
Async XLA Ops:
  0.6 7.9 %copy-start.3 = (f32[4,3,1024]{2,0,1:T(4,128)S(1)}, f32[4,3,1024]{2,0,1:T(4,128)}, u32[]{:S(2)}) copy-start(f32[4,3,1024]{2,0,1:T(4,128)} %param.11) | copy-start | bytes 147460
  1.5 7.0 %copy-start.4 = (f32[1024]{0:T(1024)S(1)}, f32[1024]{0:T(1024)}, u32[]{:S(2)}) copy-start(f32[1024]{0:T(1024)} %param.13) | copy-start | bytes 12292
  1.6 8.7 %collective-permute-start.1 = (f32[4,4,1024]{2,1,0:T(4,128)S(1)}, f32[4,4,1024]{2,1,0:T(4,128)S(1)}, u32[]{:S(2)}, u32[]{:S(2)}) collective-permute-start(f32[4,4,1024]{2,1,0:T(4,128)S(1)} %pad_select_fusion.own_ref), channel_id=1, source_target_pairs={{0,1},{1,0},{2,3},{3,2},{4,5},{5,4},{6,7},{7,6},{8,9},{9,8},{10,11... | collective-permute-start | bytes 196616 | tf_op jit(solution)/shard_map/ppermute | solution.py:374
  3.8 6.5 %collective-permute-start = (f32[4,4,1024]{2,1,0:T(4,128)S(1)}, f32[4,4,1024]{2,1,0:T(4,128)S(1)}, u32[]{:S(2)}, u32[]{:S(2)}) collective-permute-start(f32[4,4,1024]{2,1,0:T(4,128)S(1)} %pad_select_fusion.own_ref), channel_id=1, source_target_pairs={{0,15},{1,2},{2,1},{3,4},{4,3},{5,6},{6,5},{7,8},{8,7},{9,10},{10,... | collective-permute-start | bytes 196616 | tf_op jit(solution)/shard_map/ppermute | solution.py:373
  10.3 20.9 %copy-start = (bf16[768,256]{1,0:T(8,128)(2,1)S(1)}, bf16[768,256]{1,0:T(8,128)(2,1)}, u32[]{:S(2)}) copy-start(bf16[768,256]{1,0:T(8,128)(2,1)} %constant.13.clone.low_ref) | copy-start | bytes 1179652
  10.3 20.9 %copy-start.1 = (bf16[768,256]{1,0:T(8,128)(2,1)S(1)}, bf16[768,256]{1,0:T(8,128)(2,1)}, u32[]{:S(2)}) copy-start(bf16[768,256]{1,0:T(8,128)(2,1)} %constant.12.clone.mid_ref) | copy-start | bytes 1179652
  10.3 20.9 %copy-start.2 = (bf16[768,256]{1,0:T(8,128)(2,1)S(1)}, bf16[768,256]{1,0:T(8,128)(2,1)}, u32[]{:S(2)}) copy-start(bf16[768,256]{1,0:T(8,128)(2,1)} %constant.11.clone.high_ref) | copy-start | bytes 1179652

commit v4 on v3

--- a/solution.py
+++ b/solution.py
@@ -113,10 +113,10 @@
         m0 = jnp.where(last, 0.0, m)
         l0 = jnp.where(last, 0.0, l)
         norms = jnp.concatenate([h[3:4], m[3:4], l[3:4], jnp.zeros((1, ATOM_DEV), jnp.float32)], 0)
-        left = jnp.concatenate([h1, h1, h1, m0, m0, l0, norms, jnp.zeros_like(h)], 0)
+        left = jnp.concatenate([h1, h1, h1, m0, m0, l0, norms, jnp.zeros_like(h)], 0).astype(jnp.bfloat16)
         for tile in range(TILE_DEV):
             lanes = slice(tile * TILE, (tile + 1) * TILE)
-            left_ref[tile, bead] = left[:, lanes].T.astype(jnp.bfloat16)
+            left_ref[tile, bead] = left[:, lanes]
 
 
 def fetches(refs, plan_refs, sems):
@@ -150,7 +150,6 @@
 
 def add_slots(size, list_ref, left_ref, right_ref, value_ref, acc_ref):
     spare = list_ref.shape[0] // 2
-    dims = (((1,), (1,)), ((), ()))
 
     def one_group(start, slots):
         exponents, sums = [], []
@@ -159,8 +158,11 @@
             other = list_ref[spare + start + slot]
             source = jnp.minimum(tile, TILE_DEV - 1)
             for bead in range(BEAD_DEV):
-                exponent = jnp.dot(
-                    left_ref[source, bead], right_ref[other, bead], preferred_element_type=jnp.float32
+                exponent = lax.dot_general(
+                    right_ref[other, bead],
+                    left_ref[source, bead],
+                    (((0,), (0,)), ((), ())),
+                    preferred_element_type=jnp.float32,
                 )
                 exponents.append((tile, other, bead, exponent))
         for tile, other, bead, exponent in exponents:
@@ -168,10 +170,9 @@
             high = weight.astype(jnp.bfloat16)
             low = (weight - high.astype(jnp.float32)).astype(jnp.bfloat16)
             value = value_ref[other, bead]
-            total = lax.dot_general(
+            total = jnp.dot(
                 jnp.concatenate([value, value], 1),
-                jnp.concatenate([high, low], 1),
-                dims,
+                jnp.concatenate([high, low], 0),
                 preferred_element_type=jnp.float32,
             )
             sums.append((tile, bead, total))
@@ -320,7 +321,7 @@
         functools.partial(near_kernel, tiles),
         out_shape=(
             f32(TILE_DEV + 1, BEAD_DEV, 16, TILE),
-            bf16(TILE_DEV, BEAD_DEV, TILE, 32),
+            bf16(TILE_DEV, BEAD_DEV, 32, TILE),
             f32(ROWS, ATOM_DEV),
             f32(ROWS, ATOM_DEV),
             *(jax.ShapeDtypeStruct(part.shape, part.dtype) for part in plan[:2]),

time: 45.2 us -> 44.2 us (0.978); the launches traced: 44.3 us -> 44.2 us
  transfers between devices with their start and end apart: 2 -> 2, of which waited for: 0 -> 1; matrix products, arithmetic and copies ran while one was open for 0% -> 0% of each run, Pallas kernels for 4% -> 3%
where the time goes in v4:
time: 44.2 us
  blocking collectives  31.1 us (70%)
  starting transfers between devices  6.31 us (14%)
  Pallas kernels  4.26 us (10%)
  between operations  1.36 us (3%)
  other arithmetic  0.9 us (2%)
    all_to_all x1, blocking collectives, on_device(): x = lax.all_to_all(sent, 'bead', 0, 0, tiled=True)  19.5 us
    all_to_all x1, blocking collectives, on_device(): y = lax.all_to_all(y, 'bead', 0, 0, tiled=True)  11.6 us
    ppermute x1, starting transfers between devices, on_device(): lax.ppermute(own, 'atom', [(i, (i + 1 if i % 2 else i - 1) % blocks) for...  4.1 us
    ppermute x1, starting transfers between devices, on_device(): first = lax.ppermute(own, 'atom', [(i, i ^ 1) for i in range(blocks)])  2.21 us
    pallas_call x1, Pallas kernels, near_forces(): pl.pallas_call(functools.partial(near_kernel, tiles), out_shape=(f32(TILE...  1.42 us
    pallas_call x1, Pallas kernels, far_forces(): pl.pallas_call(functools.partial(far_kernel, tiles), out_shape=f32(peers,...  1.41 us
    select_n x1, other arithmetic, pack(): jnp.where(axis < 3, jnp.pad(positions, ((0, 1), (0, 0), (0, 0))), charge[...  0.89 us
  transfers between devices with their start and end apart: 2, of which 1 were waited for; matrix products, arithmetic and copies ran while one was open for 0% of the time, Pallas kernels for 3%

profile of v4, /device:TPU:1, one launch (start us, length us, event | category | flops | bytes accessed | tf_op | source)
XLA Modules:
  0.0 44.2 jit_solution(11781874065421053725)
XLA Ops:
  0.6 0.0 copy-start.3
  0.7 0.9 %pad_select_fusion.own_ref = f32[4,4,1024]{2,1,0:T(4,128)S(1)} fusion(f32[3,4,1024]{2,1,0:T(4,128)} %bitcast.8, f32[1024]{0:T(1024)} %param.12, pred[4]{0:T(512)(128)(4,1)S(1)} %iota_compare_fusion), kind=kLoop, calls=%fused_computation | loop fusion | flops 16384 | bytes 118788 | tf_op jit(solution)/shard_map/jit(_where)/select_n | solution.py:301
  1.5 0.0 copy-start.4
  1.6 2.2 %collective-permute-start.1 = (f32[4,4,1024]{2,1,0:T(4,128)S(1)}, f32[4,4,1024]{2,1,0:T(4,128)S(1)}, u32[]{:S(2)}, u32[]{:S(2)}) collective-permute-start(f32[4,4,1024]{2,1,0:T(4,128)S(1)} %pad_select_fusion.own_ref), channel_id=1, source_target_pairs={{0,1},{1,0},{2,3},{3,2},{4,5},{5,4},{6,7},{7,6},{8,9},{9,8},{10,11... | collective-permute-start | bytes 196616 | tf_op jit(solution)/shard_map/ppermute | solution.py:375
  3.8 4.1 %collective-permute-start = (f32[4,4,1024]{2,1,0:T(4,128)S(1)}, f32[4,4,1024]{2,1,0:T(4,128)S(1)}, u32[]{:S(2)}, u32[]{:S(2)}) collective-permute-start(f32[4,4,1024]{2,1,0:T(4,128)S(1)} %pad_select_fusion.own_ref), channel_id=1, source_target_pairs={{0,15},{1,2},{2,1},{3,4},{4,3},{5,6},{6,5},{7,8},{8,7},{9,10},{10,... | collective-permute-start | bytes 196616 | tf_op jit(solution)/shard_map/ppermute | solution.py:374
  8.5 0.0 copy-done.3
  8.5 0.0 copy-done.4
  8.5 1.4 %shard_map.121 = (f32[9,4,16,128]{3,2,1,0:T(8,128)S(1)}, bf16[8,4,32,128]{3,2,1,0:T(8,128)(2,1)S(1)}, f32[16,1024]{1,0:T(8,128)S(1)}, f32[16,1024]{1,0:T(8,128)S(1)}, s32[32]{0:T(128)S(1)}, /*index=5*/s32[32]{0:T(128)S(1)}) custom-call(s32[32]{0:T(128)} %local_ref.1, s32[32]{0:T(128)} %other_ref.1, s32[1]{0:T(128)S(6)} %copy.13.count_ref, ...), custom_call_target="tpu_custom_call" | custom-call | tf_op jit(solution)/shard_map/pallas_call | solution.py:320
  10.0 0.0 collective-permute-done.1.first_ref
  10.0 0.2 collective-permute-done.second_ref
  10.2 0.0 copy-start
  10.2 0.0 copy-start.1
  10.2 0.0 copy-start.2
  10.2 1.4 %shard_map.122 = f32[16,16,128]{2,1,0:T(8,128)S(1)} custom-call(s32[32]{0:T(128)S(1)} %get-tuple-element.12.local_ref, s32[32]{0:T(128)S(1)} %get-tuple-element.13.other_ref, s32[1]{0:T(128)S(6)} %copy.13.count_ref, f32[16,1024]{1,0:T(8,128)S(1)} %get-tuple-element.14.own_ref, f32[4,4,1024]{2,1,0:T(4,128)S(1)} %collective-permute-done.second_ref, ...), custom_call_target="tpu_custom_call" | custom-call | tf_op jit(solution)/shard_map/pallas_call | solution.py:337
  11.6 19.5 %all_to_all.10.x_ref = f32[16,16,128]{2,1,0:T(8,128)S(1)} all-to-all(f32[16,16,128]{2,1,0:T(8,128)S(1)} %shard_map.122), channel_id=1, replica_groups=mesh['bead'=16,'atom'=16] {'bead'}, dimensions={0} | all-to-all | bytes 262144 | tf_op jit(solution)/shard_map/all_to_all | solution.py:381
  31.2 0.0 copy-done
  31.2 0.0 copy-done.1
  31.2 0.0 copy-done.2
  31.2 0.7 %shard_map.123 = f32[16,16,128]{2,1,0:T(8,128)S(1)} custom-call(f32[16,16,128]{2,1,0:T(8,128)S(1)} %all_to_all.10.x_ref, bf16[768,256]{1,0:T(8,128)(2,1)S(1)} %copy-done.2, bf16[768,256]{1,0:T(8,128)(2,1)S(1)} %copy-done.1, bf16[768,256]{1,0:T(8,128)(2,1)S(1)} %copy-done), custom_call_target="tpu_custom_call" | custom-call | tf_op jit(solution)/shard_map/pallas_call | solution.py:351
  31.9 11.6 %all_to_all.11.y_ref = f32[16,16,128]{2,1,0:T(8,128)S(1)} all-to-all(f32[16,16,128]{2,1,0:T(8,128)S(1)} %shard_map.123), channel_id=1, replica_groups=mesh['bead'=16,'atom'=16] {'bead'}, dimensions={0} | all-to-all | bytes 262144 | tf_op jit(solution)/shard_map/all_to_all | solution.py:383
  43.5 0.8 %shard_map.124 = (f32[3,4,1024]{2,1,0:T(4,128)}, f32[3,4,1024]{2,1,0:T(4,128)}, f32[1,1024]{1,0:T(1,128)}) custom-call(f32[16,16,128]{2,1,0:T(8,128)S(1)} %all_to_all.11.y_ref), custom_call_target="tpu_custom_call" | custom-call | tf_op jit(solution)/shard_map/pallas_call | solution.py:357
  (1 shorter events, 0.0 us)
Async XLA Ops:
  0.6 7.9 %copy-start.3 = (f32[4,3,1024]{2,0,1:T(4,128)S(1)}, f32[4,3,1024]{2,0,1:T(4,128)}, u32[]{:S(2)}) copy-start(f32[4,3,1024]{2,0,1:T(4,128)} %param.11) | copy-start | bytes 147460
  1.5 7.0 %copy-start.4 = (f32[1024]{0:T(1024)S(1)}, f32[1024]{0:T(1024)}, u32[]{:S(2)}) copy-start(f32[1024]{0:T(1024)} %param.13) | copy-start | bytes 12292
  1.6 8.4 %collective-permute-start.1 = (f32[4,4,1024]{2,1,0:T(4,128)S(1)}, f32[4,4,1024]{2,1,0:T(4,128)S(1)}, u32[]{:S(2)}, u32[]{:S(2)}) collective-permute-start(f32[4,4,1024]{2,1,0:T(4,128)S(1)} %pad_select_fusion.own_ref), channel_id=1, source_target_pairs={{0,1},{1,0},{2,3},{3,2},{4,5},{5,4},{6,7},{7,6},{8,9},{9,8},{10,11... | collective-permute-start | bytes 196616 | tf_op jit(solution)/shard_map/ppermute | solution.py:375
  3.8 6.4 %collective-permute-start = (f32[4,4,1024]{2,1,0:T(4,128)S(1)}, f32[4,4,1024]{2,1,0:T(4,128)S(1)}, u32[]{:S(2)}, u32[]{:S(2)}) collective-permute-start(f32[4,4,1024]{2,1,0:T(4,128)S(1)} %pad_select_fusion.own_ref), channel_id=1, source_target_pairs={{0,15},{1,2},{2,1},{3,4},{4,3},{5,6},{6,5},{7,8},{8,7},{9,10},{10,... | collective-permute-start | bytes 196616 | tf_op jit(solution)/shard_map/ppermute | solution.py:374
  10.2 21.0 %copy-start = (bf16[768,256]{1,0:T(8,128)(2,1)S(1)}, bf16[768,256]{1,0:T(8,128)(2,1)}, u32[]{:S(2)}) copy-start(bf16[768,256]{1,0:T(8,128)(2,1)} %constant.13.clone.low_ref) | copy-start | bytes 1179652
  10.2 21.0 %copy-start.1 = (bf16[768,256]{1,0:T(8,128)(2,1)S(1)}, bf16[768,256]{1,0:T(8,128)(2,1)}, u32[]{:S(2)}) copy-start(bf16[768,256]{1,0:T(8,128)(2,1)} %constant.12.clone.mid_ref) | copy-start | bytes 1179652
  10.2 21.0 %copy-start.2 = (bf16[768,256]{1,0:T(8,128)(2,1)S(1)}, bf16[768,256]{1,0:T(8,128)(2,1)}, u32[]{:S(2)}) copy-start(bf16[768,256]{1,0:T(8,128)(2,1)} %constant.11.clone.high_ref) | copy-start | bytes 1179652

commit v5 on v4

--- a/solution.py
+++ b/solution.py
@@ -273,11 +273,12 @@
     out_ref[...] = jnp.where(comp == 3, spring, moved).reshape(out_ref.shape)
 
 
-def unpack_kernel(y_ref, pos_ref, mom_ref, spring_ref):
+def unpack_kernel(y_ref, pos_hbm, mom_hbm, spring_ref, pos_ref, mom_ref, sems):
     lane = lax.broadcasted_iota(jnp.int32, (BEAD_DEV, TILE), 1)
-    for tile in range(TILE_DEV):
-        lanes = slice(tile * TILE, (tile + 1) * TILE)
-        for axis in range(4):
+    copies = []
+    for axis in range(4):
+        for tile in range(TILE_DEV):
+            lanes = slice(tile * TILE, (tile + 1) * TILE)
             rows = pl.ds(axis, BEAD_DEV, stride=4)
             first, second = y_ref[2 * tile, rows, :], y_ref[2 * tile + 1, rows, :]
             place = jnp.where(lane < HALF, first, pltpu.roll(second, HALF, 1))
@@ -286,6 +287,13 @@
             else:
                 pos_ref[axis, :, lanes] = place
                 mom_ref[axis, :, lanes] = jnp.where(lane < HALF, pltpu.roll(first, HALF, 1), second)
+        if axis < 3:
+            copies.append(pltpu.make_async_copy(pos_ref.at[axis], pos_hbm.at[axis], sems.at[axis]))
+            copies.append(pltpu.make_async_copy(mom_ref.at[axis], mom_hbm.at[axis], sems.at[3 + axis]))
+            for copy in copies[-2:]:
+                copy.start()
+    for copy in copies:
+        copy.wait()
 
 
 def f32(*shape):
@@ -358,7 +366,8 @@
         unpack_kernel,
         out_shape=(f32(3, BEAD_DEV, ATOM_DEV), f32(3, BEAD_DEV, ATOM_DEV), f32(1, ATOM_DEV)),
         in_specs=[VMEM],
-        out_specs=(VMEM,) * 3,
+        out_specs=(HBM, HBM, VMEM),
+        scratch_shapes=[pltpu.VMEM((3, BEAD_DEV, ATOM_DEV), jnp.float32)] * 2 + [pltpu.SemaphoreType.DMA((6,))],
         compiler_params=PARAMS,
     )(y)
 

time: 44.2 us -> 45 us (1.018); the launches traced: 44.2 us -> 44.3 us
  waiting for transfers between devices: 0.23 us -> 0.72 us
    pallas_call x1, Pallas kernels: 0.75 us -> 1.37 us  [unpack(): pl.pallas_call(unpack_kernel, out_shape=(f32(3, BEAD_DEV, ATOM_DEV), f32(...]
    ppermute x1, waiting for transfers between devices: 0.23 us -> 0.72 us  [on_device(): lax.ppermute(own, 'atom', [(i, (i + 1 if i % 2 else i - 1) % blocks) for...]
    pallas_call x1, Pallas kernels: 1.42 us -> 0.93 us  [near_forces(): pl.pallas_call(functools.partial(near_kernel, tiles), out_shape=(f32(TILE...]
    pallas_call x1, Pallas kernels: 1.41 us -> 0.92 us  [far_forces(): pl.pallas_call(functools.partial(far_kernel, tiles), out_shape=f32(peers,...]
  transfers between devices with their start and end apart: 2 -> 2, of which waited for: 1 -> 1; matrix products, arithmetic and copies ran while one was open for 0% -> 0% of each run, Pallas kernels for 3% -> 2%
where the time goes in v5:
time: 45 us; the launch traced here: 44.3 us
  blocking collectives  31.1 us (69%)
  starting transfers between devices  6.31 us (14%)
  Pallas kernels  3.9 us (9%)
  between operations  1.36 us (3%)
  other arithmetic  0.9 us (2%)
  waiting for transfers between devices  0.72 us (2%)
    all_to_all x1, blocking collectives, on_device(): x = lax.all_to_all(sent, 'bead', 0, 0, tiled=True)  19.5 us
    all_to_all x1, blocking collectives, on_device(): y = lax.all_to_all(y, 'bead', 0, 0, tiled=True)  11.6 us
    ppermute x1, starting transfers between devices, on_device(): lax.ppermute(own, 'atom', [(i, (i + 1 if i % 2 else i - 1) % blocks) for...  4.1 us
    ppermute x1, starting transfers between devices, on_device(): first = lax.ppermute(own, 'atom', [(i, i ^ 1) for i in range(blocks)])  2.21 us
    pallas_call x1, Pallas kernels, unpack(): pl.pallas_call(unpack_kernel, out_shape=(f32(3, BEAD_DEV, ATOM_DEV), f32(...  1.37 us
    pallas_call x1, Pallas kernels, near_forces(): pl.pallas_call(functools.partial(near_kernel, tiles), out_shape=(f32(TILE...  0.93 us
    pallas_call x1, Pallas kernels, far_forces(): pl.pallas_call(functools.partial(far_kernel, tiles), out_shape=f32(peers,...  0.92 us
  transfers between devices with their start and end apart: 2, of which 1 were waited for; matrix products, arithmetic and copies ran while one was open for 0% of the time, Pallas kernels for 2%

profile of v5, /device:TPU:1, one launch (start us, length us, event | category | flops | bytes accessed | tf_op | source)
XLA Modules:
  0.0 44.3 jit_solution(13975279861640166508)
XLA Ops:
  0.6 0.0 copy-start.3
  0.7 0.9 %pad_select_fusion.own_ref = f32[4,4,1024]{2,1,0:T(4,128)S(1)} fusion(f32[3,4,1024]{2,1,0:T(4,128)} %bitcast.8, f32[1024]{0:T(1024)} %param.12, pred[4]{0:T(512)(128)(4,1)S(1)} %iota_compare_fusion), kind=kLoop, calls=%fused_computation | loop fusion | flops 16384 | bytes 118788 | tf_op jit(solution)/shard_map/jit(_where)/select_n | solution.py:309
  1.5 0.0 copy-start.4
  1.6 2.2 %collective-permute-start.1 = (f32[4,4,1024]{2,1,0:T(4,128)S(1)}, f32[4,4,1024]{2,1,0:T(4,128)S(1)}, u32[]{:S(2)}, u32[]{:S(2)}) collective-permute-start(f32[4,4,1024]{2,1,0:T(4,128)S(1)} %pad_select_fusion.own_ref), channel_id=1, source_target_pairs={{0,1},{1,0},{2,3},{3,2},{4,5},{5,4},{6,7},{7,6},{8,9},{9,8},{10,11... | collective-permute-start | bytes 196616 | tf_op jit(solution)/shard_map/ppermute | solution.py:384
  3.8 4.1 %collective-permute-start = (f32[4,4,1024]{2,1,0:T(4,128)S(1)}, f32[4,4,1024]{2,1,0:T(4,128)S(1)}, u32[]{:S(2)}, u32[]{:S(2)}) collective-permute-start(f32[4,4,1024]{2,1,0:T(4,128)S(1)} %pad_select_fusion.own_ref), channel_id=1, source_target_pairs={{0,15},{1,2},{2,1},{3,4},{4,3},{5,6},{6,5},{7,8},{8,7},{9,10},{10,... | collective-permute-start | bytes 196616 | tf_op jit(solution)/shard_map/ppermute | solution.py:383
  8.5 0.0 copy-done.3
  8.5 0.0 copy-done.4
  8.5 0.9 %shard_map.121 = (f32[9,4,16,128]{3,2,1,0:T(8,128)S(1)}, bf16[8,4,32,128]{3,2,1,0:T(8,128)(2,1)S(1)}, f32[16,1024]{1,0:T(8,128)S(1)}, f32[16,1024]{1,0:T(8,128)S(1)}, s32[32]{0:T(128)S(1)}, /*index=5*/s32[32]{0:T(128)S(1)}) custom-call(s32[32]{0:T(128)} %local_ref.1, s32[32]{0:T(128)} %other_ref.1, s32[1]{0:T(128)S(6)} %copy.13.count_ref, ...), custom_call_target="tpu_custom_call" | custom-call | tf_op jit(solution)/shard_map/pallas_call | solution.py:328
  9.5 0.0 collective-permute-done.1.first_ref
  9.5 0.7 %collective-permute-done.second_ref = f32[4,4,1024]{2,1,0:T(4,128)S(1)} collective-permute-done((f32[4,4,1024]{2,1,0:T(4,128)S(1)}, f32[4,4,1024]{2,1,0:T(4,128)S(1)}, u32[]{:S(2)}, u32[]{:S(2)}) %collective-permute-start) | collective-permute-done | bytes 65568 | tf_op jit(solution)/shard_map/ppermute | solution.py:383
  10.2 0.0 copy-start
  10.2 0.0 copy-start.1
  10.2 0.0 copy-start.2
  10.2 0.9 %shard_map.122 = f32[16,16,128]{2,1,0:T(8,128)S(1)} custom-call(s32[32]{0:T(128)S(1)} %get-tuple-element.12.local_ref, s32[32]{0:T(128)S(1)} %get-tuple-element.13.other_ref, s32[1]{0:T(128)S(6)} %copy.13.count_ref, f32[16,1024]{1,0:T(8,128)S(1)} %get-tuple-element.14.own_ref, f32[4,4,1024]{2,1,0:T(4,128)S(1)} %collective-permute-done.second_ref, ...), custom_call_target="tpu_custom_call" | custom-call | tf_op jit(solution)/shard_map/pallas_call | solution.py:345
  11.1 19.5 %all_to_all.10.x_ref = f32[16,16,128]{2,1,0:T(8,128)S(1)} all-to-all(f32[16,16,128]{2,1,0:T(8,128)S(1)} %shard_map.122), channel_id=1, replica_groups=mesh['bead'=16,'atom'=16] {'bead'}, dimensions={0} | all-to-all | bytes 262144 | tf_op jit(solution)/shard_map/all_to_all | solution.py:390
  30.7 0.0 copy-done
  30.7 0.0 copy-done.1
  30.7 0.0 copy-done.2
  30.7 0.7 %shard_map.123 = f32[16,16,128]{2,1,0:T(8,128)S(1)} custom-call(f32[16,16,128]{2,1,0:T(8,128)S(1)} %all_to_all.10.x_ref, bf16[768,256]{1,0:T(8,128)(2,1)S(1)} %copy-done.2, bf16[768,256]{1,0:T(8,128)(2,1)S(1)} %copy-done.1, bf16[768,256]{1,0:T(8,128)(2,1)S(1)} %copy-done), custom_call_target="tpu_custom_call" | custom-call | tf_op jit(solution)/shard_map/pallas_call | solution.py:359
  31.4 11.6 %all_to_all.11.y_ref = f32[16,16,128]{2,1,0:T(8,128)S(1)} all-to-all(f32[16,16,128]{2,1,0:T(8,128)S(1)} %shard_map.123), channel_id=1, replica_groups=mesh['bead'=16,'atom'=16] {'bead'}, dimensions={0} | all-to-all | bytes 262144 | tf_op jit(solution)/shard_map/all_to_all | solution.py:392
  43.0 1.4 %shard_map.124 = (f32[3,4,1024]{2,1,0:T(4,128)}, f32[3,4,1024]{2,1,0:T(4,128)}, f32[1,1024]{1,0:T(1,128)}) custom-call(f32[16,16,128]{2,1,0:T(8,128)S(1)} %all_to_all.11.y_ref), custom_call_target="tpu_custom_call" | custom-call | tf_op jit(solution)/shard_map/pallas_call | solution.py:365
  (1 shorter events, 0.0 us)
Async XLA Ops:
  0.6 7.9 %copy-start.3 = (f32[4,3,1024]{2,0,1:T(4,128)S(1)}, f32[4,3,1024]{2,0,1:T(4,128)}, u32[]{:S(2)}) copy-start(f32[4,3,1024]{2,0,1:T(4,128)} %param.11) | copy-start | bytes 147460
  1.5 7.0 %copy-start.4 = (f32[1024]{0:T(1024)S(1)}, f32[1024]{0:T(1024)}, u32[]{:S(2)}) copy-start(f32[1024]{0:T(1024)} %param.13) | copy-start | bytes 12292
  1.6 7.9 %collective-permute-start.1 = (f32[4,4,1024]{2,1,0:T(4,128)S(1)}, f32[4,4,1024]{2,1,0:T(4,128)S(1)}, u32[]{:S(2)}, u32[]{:S(2)}) collective-permute-start(f32[4,4,1024]{2,1,0:T(4,128)S(1)} %pad_select_fusion.own_ref), channel_id=1, source_target_pairs={{0,1},{1,0},{2,3},{3,2},{4,5},{5,4},{6,7},{7,6},{8,9},{9,8},{10,11... | collective-permute-start | bytes 196616 | tf_op jit(solution)/shard_map/ppermute | solution.py:384
  3.8 6.4 %collective-permute-start = (f32[4,4,1024]{2,1,0:T(4,128)S(1)}, f32[4,4,1024]{2,1,0:T(4,128)S(1)}, u32[]{:S(2)}, u32[]{:S(2)}) collective-permute-start(f32[4,4,1024]{2,1,0:T(4,128)S(1)} %pad_select_fusion.own_ref), channel_id=1, source_target_pairs={{0,15},{1,2},{2,1},{3,4},{4,3},{5,6},{6,5},{7,8},{8,7},{9,10},{10,... | collective-permute-start | bytes 196616 | tf_op jit(solution)/shard_map/ppermute | solution.py:383
  10.2 20.5 %copy-start = (bf16[768,256]{1,0:T(8,128)(2,1)S(1)}, bf16[768,256]{1,0:T(8,128)(2,1)}, u32[]{:S(2)}) copy-start(bf16[768,256]{1,0:T(8,128)(2,1)} %constant.13.clone.low_ref) | copy-start | bytes 1179652
  10.2 20.5 %copy-start.1 = (bf16[768,256]{1,0:T(8,128)(2,1)S(1)}, bf16[768,256]{1,0:T(8,128)(2,1)}, u32[]{:S(2)}) copy-start(bf16[768,256]{1,0:T(8,128)(2,1)} %constant.12.clone.mid_ref) | copy-start | bytes 1179652
  10.2 20.5 %copy-start.2 = (bf16[768,256]{1,0:T(8,128)(2,1)S(1)}, bf16[768,256]{1,0:T(8,128)(2,1)}, u32[]{:S(2)}) copy-start(bf16[768,256]{1,0:T(8,128)(2,1)} %constant.11.clone.high_ref) | copy-start | bytes 1179652
